TPU v7x, 512 devices: a whole 4x8x8 slice. The times are simulated.
512 devices in a mesh: dp: 64 (over y, x, core), mp: 8 (over z).
Axes of the slice: x: 4, y: 8, z: 8, core: 2. Of those that a mesh axis runs over, the one named last changes fastest.
Arguments:
- up_grad: bfloat16 [64, 64, 28672], P('dp', None, 'mp'), may hold values from -60 to 60, as said below
- up_error: float32 [64, 64, 28672], P('dp', None, 'mp'), may hold values from -4 to 4
- up_warm: float32 [28672, 32], P('mp'), may hold values from -0.03125 to 0.03125
- down_grad: bfloat16 [64, 128, 8192], P('dp', None, 'mp'), may hold values from -60 to 60, as said below
- down_error: float32 [64, 128, 8192], P('dp', None, 'mp'), may hold values from -4 to 4
- down_warm: float32 [8192, 32], P('mp'), may hold values from -0.0625 to 0.0625
Outputs:
- up_average: bfloat16 [64, 28672], P(None, 'mp')
- up_residue: float32 [64, 64, 28672], P('dp', None, 'mp')
- down_average: bfloat16 [128, 8192], P(None, 'mp')
- down_residue: float32 [64, 128, 8192], P('dp', None, 'mp')
Inputs may be any that keep to these rules, and one draw needn't show every extreme that they name: `up_grad`: each replica's up gradient rows. `down_grad`: each replica's down gradient rows.
All inputs are finite; a program needn't handle non-finite values.
Results may differ from a plain program's by a relative error of at most 0.0011.
Values sent between devices are 32-bit elements; how exact they have to be, the bound alone decides.
A program may use at most 64 MiB of HBM per device.

v0:
```python
import jax
import jax.numpy as jnp
from jax import lax
from jax.sharding import PartitionSpec as P


def orthonormal(proj):
    gram = jnp.dot(proj.T, proj, precision=lax.Precision.HIGHEST)
    chol = jnp.linalg.cholesky(gram)
    return lax.linalg.triangular_solve(chol, proj, left_side=False, lower=True, transpose_a=True)


def transpose_times(merged, ortho):
    return lax.dot_general(merged, ortho, (((0,), (0,)), ((), ())), precision=lax.Precision.HIGHEST)


def expand(ortho, factor):
    return lax.dot_general(ortho, factor, (((1,), (1,)), ((), ())), precision=lax.Precision.HIGHEST)


def body(up_grad, up_error, up_warm, down_grad, down_error, down_warm):
    hi = lax.Precision.HIGHEST
    replicas = lax.axis_size("dp")
    up_merged = up_grad[0].astype(jnp.float32) + up_error[0]
    down_merged = down_grad[0].astype(jnp.float32) + down_error[0]
    up_proj = jnp.dot(up_merged, up_warm, precision=hi)
    down_proj = jnp.dot(down_merged, down_warm, precision=hi)
    up_proj, down_proj = lax.psum((up_proj, down_proj), "mp")
    up_proj, down_proj = lax.psum((up_proj, down_proj), "dp")
    up_ortho = orthonormal(up_proj)
    down_ortho = orthonormal(down_proj)
    up_back = transpose_times(up_merged, up_ortho)
    down_back = transpose_times(down_merged, down_ortho)
    up_total, down_total = lax.psum((up_back, down_back), "dp")
    up_delta = expand(up_ortho, up_total / replicas)
    down_delta = expand(down_ortho, down_total / replicas)
    up_residue = (up_merged - up_delta)[None]
    down_residue = (down_merged - down_delta)[None]
    return (
        up_delta.astype(jnp.bfloat16),
        up_residue,
        down_delta.astype(jnp.bfloat16),
        down_residue,
    )


def solution(mesh):
    return jax.shard_map(
        body,
        mesh=mesh,
        in_specs=(
            P("dp", None, "mp"),
            P("dp", None, "mp"),
            P("mp", None),
            P("dp", None, "mp"),
            P("dp", None, "mp"),
            P("mp", None),
        ),
        out_specs=(P(None, "mp"), P("dp", None, "mp"), P(None, "mp"), P("dp", None, "mp")),
        check_vma=False,
    )
```

profile of v0, /device:TPU:1, one launch (start us, length us, event | category | flops | bytes accessed | tf_op | source)
XLA Modules:
  0.0 513.1 jit_solution(1625506712716401787)
XLA Ops:
  7.2 0.0 copy-start
  7.2 0.0 copy-start.2
  7.2 0.0 copy-start.4
  7.2 0.0 copy-start.6
  7.2 0.0 all-reduce.5.cloned.1.call-start
  7.3 0.9 copy-done
  8.2 2.2 fusion.2
  10.4 0.0 copy-done.2
  10.4 0.0 copy-done.4
  10.4 0.0 copy-done.6
  10.4 0.0 copy-start.1
  10.4 0.6 fusion.7
  11.0 0.0 copy-start.3
  11.0 29.9 %all-reduce.2 = (f32[64,32]{0,1:T(8,128)S(1)}, f32[128,32]{0,1:T(8,128)S(1)}) all-reduce(f32[64,32]{0,1:T(8,128)S(1)} %fusion.2, f32[128,32]{0,1:T(8,128)S(1)} %fusion.7), channel_id=1, replica_groups=mesh['dp'=64,'mp'=8] {'mp'}, use_global_device_ids=true, to_apply=%region_0.0 | all-reduce | flops 6144 | bytes 49152 | tf_op jit(solution)/shard_map/psum | solution.py:28
  40.9 248.9 %all-reduce = (f32[64,32]{0,1:T(8,128)S(1)}, f32[128,32]{0,1:T(8,128)S(1)}) all-reduce(f32[64,32]{0,1:T(8,128)S(1)} %get-tuple-element.9, f32[128,32]{0,1:T(8,128)S(1)} %get-tuple-element.10), channel_id=1, replica_groups=mesh['dp'=64,'mp'=8] {'dp'}, use_global_device_ids=true, to_apply=%region_1.0 | all-reduce | flops 6144 | bytes 49152 | tf_op jit(solution)/shard_map/psum | solution.py:29
  289.8 0.1 fusion.30
  290.0 0.1 fusion.31
  290.1 0.1 copy.13
  290.2 2.9 cholesky.55
  293.1 0.6 compare_reduce_fusion
  293.8 0.7 fusion.17
  294.5 2.4 custom-call.9
  296.9 0.2 fusion.18
  297.1 0.1 copy.12
  297.2 2.9 cholesky.44
  300.2 0.6 compare_reduce_fusion.1
  300.8 0.7 fusion.16
  301.5 2.4 custom-call.8
  303.9 0.2 fusion.21
  304.1 0.0 copy-done.1
  304.2 0.0 copy-done.3
  304.2 1.5 fusion
  305.6 1.8 fusion.5
  307.4 0.0 all-reduce.5.cloned.1.call-update
  307.4 194.2 %all-reduce.5.cloned.1.call-done = (f32[3584,32]{0,1:T(8,128)}, f32[1024,32]{1,0:T(8,128)}) async-done(((f32[3584,32]{0,1:T(8,128)}, f32[1024,32]{1,0:T(8,128)}), (f32[3584,32]{0,1:T(8,128)}, f32[1024,32]{1,0:T(8,128)})) %all-reduce.5.cloned.1.call-update) | async-done | bytes 589840 | tf_op jit(solution)/shard_map/psum | solution.py:34
  501.6 0.0 copy-start.5
  501.6 2.6 fusion.9
  504.2 0.0 copy-done.5
  504.2 2.0 fusion.4
  (4 shorter events, 0.1 us)
Async XLA Ops:
  7.2 1.0 copy-start
  7.2 3.2 copy-start.2
  7.2 3.2 copy-start.4
  7.2 3.2 copy-start.6
  7.2 494.4 %all-reduce.5.cloned.1.call-start = ((), (), s32[]{:S(2)}) async-start(), calls=%async_computation | async-start | bytes 1966080 | tf_op jit(solution)/shard_map/psum | solution.py:34
  10.4 293.8 %copy-start.1 = (f32[1,64,3584]{2,1,0:T(8,128)S(1)}, f32[1,64,3584]{2,1,0:T(8,128)}, u32[]{:S(2)}) copy-start(f32[1,64,3584]{2,1,0:T(8,128)} %param.8) | copy-start | bytes 2752516
  11.0 293.1 %copy-start.3 = (bf16[1,64,3584]{2,1,0:T(8,128)(2,1)S(1)}, bf16[1,64,3584]{2,1,0:T(8,128)(2,1)}, u32[]{:S(2)}) copy-start(bf16[1,64,3584]{2,1,0:T(8,128)(2,1)} %param.7) | copy-start | bytes 1376260
  501.6 2.6 copy-start.5
Sparse Core Ops, SparseCore 0:
  307.6 193.9 all-reduce.4
where the time goes:
time: 515 us; the launch traced here: 513 us
  blocking collectives  279 us (54%)
  waiting for transfers between devices  194 us (38%)
  between operations  14.2 us (3%)
  other arithmetic  13.4 us (3%)
  matrix products  11.4 us (2%)
    psum x1, blocking collectives, body(): up_proj, down_proj = lax.psum((up_proj, down_proj), 'dp')  249 us
    psum x1, waiting for transfers between devices, body(): up_total, down_total = lax.psum((up_back, down_back), 'dp')  194 us
    psum x1, blocking collectives, body(): up_proj, down_proj = lax.psum((up_proj, down_proj), 'mp')  29.9 us
  transfers between devices with their start and end apart: 1, of which 1 were waited for; matrix products, arithmetic and copies ran while one was open for 0% of the time, Pallas kernels for 0%

commit v1 on v0

v1 whole, which is shorter than its diff:
```python
import jax
import jax.numpy as jnp
from jax import lax
from jax.experimental import pallas as pl
from jax.experimental.pallas import tpu as pltpu
from jax.sharding import PartitionSpec as P

F32 = jnp.float32
BF16 = jnp.bfloat16
HI = lax.Precision.HIGHEST
MESH = pl.DeviceIdType.MESH
NY, NX, NC, NZ = 8, 4, 2, 8
RANK = 32
UP_R, UP_C = 64, 3584
DN_R, DN_C = 128, 1024
HALF = UP_C // 2
SH = 48
FR = 24


def nt(a, b, precision=None):
    return lax.dot_general(a, b, (((1,), (1,)), ((), ())), preferred_element_type=F32, precision=precision)


def split(a):
    hi = a.astype(BF16)
    return hi, (a - hi.astype(F32)).astype(BF16)


def nt3(a, b):
    ah, al = split(a)
    bh, bl = split(b)
    return nt(ah, bh) + nt(ah, bl) + nt(al, bh)


def eliminate(a1, a2):
    shape = (RANK, 128)
    row = lax.broadcasted_iota(jnp.int32, shape, 0)
    lane = lax.broadcasted_iota(jnp.int32, shape, 1)
    in_dn = lane >= 96
    scale_u = jnp.ones(shape, F32)
    scale_d = jnp.ones(shape, F32)
    for panel in range(4):
        first = panel * 8
        cu = [jnp.broadcast_to(a1[:, 64 + first + m:65 + first + m], shape) for m in range(8)]
        cd = [jnp.broadcast_to(a1[:, 96 + first + m:97 + first + m], shape) for m in range(8)]
        for m in range(8):
            k = first + m
            below = row > k
            pu = cu[m][k:k + 1, :]
            pd = cd[m][k:k + 1, :]
            fu = jnp.where(below, cu[m] * (1.0 / pu), 0.0)
            fd = jnp.where(below, cd[m] * (1.0 / pd), 0.0)
            for n in range(m + 1, 8):
                cu[n] = cu[n] - fu * cu[n][k:k + 1, :]
                cd[n] = cd[n] - fd * cd[n][k:k + 1, :]
            a1 = a1 - jnp.where(in_dn, fd, fu) * a1[k:k + 1, :]
            a2 = a2 - fd * a2[k:k + 1, :]
            scale_u = jnp.where(row == k, lax.rsqrt(pu), scale_u)
            scale_d = jnp.where(row == k, lax.rsqrt(pd), scale_d)
    return a1 * scale_u, a2 * scale_d


def exchange(ug, ue, uw, dg, de, dw, f_out, wu_out, wd_out,
             vug, vue, vuw, vdg, vde, vdw, T, Rc, Rx, Ry, FG,
             pt, pc, px, pxr, pz, py, pg,
             in_sem, s_mc, r_mc, s_mx, r_mx, s_my, r_my,
             s_pc, r_pc, s_px, r_px, s_pz, r_pz, s_py, r_py, s_pa, r_pa, s_pb, r_pb,
             s_fy, r_fy, s_fx, r_fx, s_fc, r_fc, out_sem):
    d = lax.axis_index("dp")
    z = lax.axis_index("mp")
    c = lax.rem(d, 2)
    x = lax.rem(lax.div(d, 2), NX)
    y = lax.div(d, 8)

    def at(yy, xx, cc):
        return ((yy * NX + xx) * NC + cc, z)

    partner = at(y, x, 1 - c)

    def xpeer(o):
        return at(y, lax.rem(x + o, NX), c)

    def ypeer(o):
        return at(lax.rem(y + o, NY), x, c)

    def zpeer(o):
        return (d, lax.rem(z + o, NZ))

    bar = pltpu.get_barrier_semaphore()
    pl.semaphore_signal(bar, 1, device_id=partner, device_id_type=MESH)
    for o in range(1, NZ):
        pl.semaphore_signal(bar, 1, device_id=zpeer(o), device_id_type=MESH)
    for o in range(1, NY):
        pl.semaphore_signal(bar, 1, device_id=ypeer(o), device_id_type=MESH)
    for o in range(1, NX):
        pl.semaphore_signal(bar, 1, device_id=xpeer(o), device_id_type=MESH)

    loads = [pltpu.make_async_copy(a, b, in_sem.at[i])
             for i, (a, b) in enumerate([(ug, vug), (ue, vue), (uw, vuw), (dg, vdg), (de, vde), (dw, vdw)])]
    for cp in loads:
        cp.start()

    for cp in loads[:3]:
        cp.wait()
    acc = jnp.zeros((RANK, UP_R), F32)
    for b in range(HALF // 256):
        parts = []
        for half in range(2):
            cols = pl.ds(half * HALF + 256 * b, 256)
            m = vug[:, cols].astype(F32) + vue[:, cols]
            acc += nt3(vuw[:, cols], m)
            parts.append(m)
        stacked = jnp.concatenate(parts, axis=0)
        for s in range(2):
            turned = stacked[:, 128 * s:128 * (s + 1)].T
            for i in range(16):
                tile = (2 * b + s) * 16 + i
                q, u = tile // 7, tile % 7
                rows = turned[8 * i:8 * i + 8, :]
                if u <= 3:
                    T[0, q // NY, q % NY, 8 * u:8 * u + 8, :] = rows
                if u >= 3:
                    T[1, q // NY, q % NY, 8 * (u - 3):8 * (u - 3) + 8, :] = rows
    pt[0:32, :] = jnp.concatenate([acc, jnp.zeros((RANK, 64), F32)], axis=1)
    for cp in loads[3:]:
        cp.wait()
    acc = jnp.zeros((RANK, DN_R), F32)
    for b in range(DN_C // 256):
        cols = pl.ds(256 * b, 256)
        m = vdg[:, cols].astype(F32) + vde[:, cols]
        acc += nt3(vdw[:, cols], m)
        for s in range(2):
            turned = m[:, 128 * s:128 * (s + 1)].T
            for i in range(16):
                tile = (2 * b + s) * 16 + i
                q, u = tile // 4, tile % 4
                T[u // 2, q // NY, q % NY, 32 + 8 * (u % 2):40 + 8 * (u % 2), :] = turned[8 * i:8 * i + 8, :]
    pt[32:64, :] = acc

    pl.semaphore_wait(bar, 1 + 7 + 7 + 3)

    def remote(src, dst, ssem, rsem, dev):
        cp = pltpu.make_async_remote_copy(src_ref=src, dst_ref=dst, send_sem=ssem, recv_sem=rsem,
                                          device_id=dev, device_id_type=MESH)
        cp.start()
        return cp

    sent = []
    cp_pc = remote(pt.at[pl.ds((1 - c) * 32, 32)], pc, s_pc, r_pc, partner)
    sent.append(cp_pc)
    order = [1, 3, 2, 0]
    cp_mc = {}
    for o in order:
        xx = lax.rem(x + o, NX)
        cp_mc[o] = remote(T.at[1 - c, xx], Rc.at[xx], s_mc.at[o], r_mc.at[o], partner)
        sent.append(cp_mc[o])
    cp_pc.wait_recv()
    px[...] = pt[pl.ds(pl.multiple_of(c * 32, 32), 32), :] + pc[...]
    cp_px = [remote(px.at[pl.ds(lax.rem(x + o, NX) * 8, 8)], pxr.at[o - 1], s_px.at[o - 1], r_px.at[o - 1], xpeer(o))
             for o in (1, 2, 3)]
    sent += cp_px
    cp_mx = []
    for o in order:
        xx = lax.rem(x + o, NX)
        cp_mc[o].wait_recv()
        T[c, xx] = T[c, xx] + Rc[xx]
        if o:
            cp_mx.append(remote(T.at[c, xx], Rx.at[o - 1], s_mx.at[o - 1], r_mx.at[o - 1], xpeer(o)))
    sent += cp_mx
    for cp in cp_px:
        cp.wait_recv()
    pz[z] = (px[pl.ds(pl.multiple_of(x * 8, 8), 8), :] + pxr[0]) + (pxr[1] + pxr[2])
    cp_pz = [remote(pz.at[z], pz.at[z], s_pz.at[o - 1], r_pz.at[o - 1], zpeer(o)) for o in range(1, NZ)]
    sent += cp_pz
    for cp in cp_pz:
        cp.wait_recv()
    py[y] = ((pz[0] + pz[1]) + (pz[2] + pz[3])) + ((pz[4] + pz[5]) + (pz[6] + pz[7]))
    cp_py = [remote(py.at[y], py.at[y], s_py.at[o - 1], r_py.at[o - 1], ypeer(o)) for o in range(1, NY)]
    sent += cp_py
    for cp in cp_py:
        cp.wait_recv()
    mine = pl.ds(pl.multiple_of(x * 8, 8), 8)
    pg[c, mine, :] = ((py[0] + py[1]) + (py[2] + py[3])) + ((py[4] + py[5]) + (py[6] + py[7]))
    cp_pa = [remote(pg.at[c, mine], pg.at[c, mine], s_pa.at[o - 1], r_pa.at[o - 1], xpeer(o)) for o in (1, 2, 3)]
    sent += cp_pa

    for cp in cp_mx:
        cp.wait_recv()
    cp_my = []
    for o in (4, 3, 5, 2, 6, 1, 7, 0):
        yy = lax.rem(y + o, NY)
        T[c, x, yy] = (T[c, x, yy] + Rx[0, yy]) + (Rx[1, yy] + Rx[2, yy])
        if o:
            cp_my.append(remote(T.at[c, x, yy], Ry.at[o - 1], s_my.at[o - 1], r_my.at[o - 1], ypeer(o)))
    sent += cp_my

    for cp in cp_pa:
        cp.wait_recv()
    cp_pb = remote(pg.at[c], pg.at[c], s_pb, r_pb, partner)
    sent.append(cp_pb)
    cp_pb.wait_recv()

    a1 = pg[0]
    a2 = pg[1]
    gu = nt(a1, a1, HI)
    gd = nt(a2, a2, HI)
    a1, a2 = eliminate(jnp.concatenate([a1[:, :64], gu, gd], axis=1), a2)
    lane = lax.broadcasted_iota(jnp.int32, (RANK, 128), 1)
    left = jnp.where(lane < 64, a1, 0.0)
    right = pltpu.roll(left, 64, axis=1)
    wu = jnp.concatenate([left, right, left, right], axis=0)
    wd = jnp.concatenate([a2, a2, a2, a2], axis=0)
    wu_out[...] = wu.T
    wd_out[...] = wd.T

    for cp in cp_my:
        cp.wait_recv()
    shard = T[c, x, y]
    for o in range(1, NY):
        shard = shard + Ry[o - 1]
    shard = shard * (1.0 / 64.0)
    ru = nt(shard[0:32], wu, HI)
    rd = nt(shard[32:48], wd, HI)
    lane16 = lax.broadcasted_iota(jnp.int32, (16, 128), 1)
    FG[c, x, y, 0:16, :] = jnp.where(lane16 < 64, ru[0:16], ru[16:32])
    FG[c, x, y, 16:24, :] = jnp.where(lane16[0:8] < 32, rd[0:8], rd[8:16])

    cp_fy = [remote(FG.at[c, x, y], FG.at[c, x, y], s_fy.at[o - 1], r_fy.at[o - 1], ypeer(o)) for o in (4, 3, 5, 2, 6, 1, 7)]
    sent += cp_fy
    for cp in cp_fy:
        cp.wait_recv()
    cp_fx = [remote(FG.at[c, x], FG.at[c, x], s_fx.at[o - 1], r_fx.at[o - 1], xpeer(o)) for o in (2, 1, 3)]
    sent += cp_fx
    cp_fc = [remote(FG.at[c, x], FG.at[c, x], s_fc.at[0], r_fc.at[0], partner)]
    for cp, o in zip(cp_fx, (2, 1, 3)):
        cp.wait_recv()
        xx = lax.rem(x - o + NX, NX)
        cp_fc.append(remote(FG.at[c, xx], FG.at[c, xx], s_fc.at[o], r_fc.at[o], partner))
    sent += cp_fc
    for cp in cp_fc:
        cp.wait_recv()
    cp_out = pltpu.make_async_copy(FG, f_out, out_sem)
    cp_out.start()
    for cp in sent:
        cp.wait_send()
    cp_out.wait()


def finish(f, wu, wd, ug, ue, dg, de, ua, ur, da, dr, fu, fd):
    lane = lax.broadcasted_iota(jnp.int32, (8, 128), 1)
    for tile in range(HALF // 8):
        q, u = tile // 7, tile % 7
        core, s = (0, u) if u <= 3 else (1, u - 3)
        r0 = (s % 2) * 8
        rows = f[core, q // NY, q % NY, r0:r0 + 8, :]
        fu[8 * tile:8 * tile + 8, :] = jnp.where(lane // 64 == s // 2, rows, 0.0)
    for tile in range(DN_C // 8):
        q, u = tile // 4, tile % 4
        rows = f[u // 2, q // NY, q % NY, 16:24, :]
        fd[8 * tile:8 * tile + 8, :] = jnp.where(lane // 32 == u % 2, rows, 0.0)
    for b in range(HALF // 256):
        delta = nt3(wu[...], fu[256 * b:256 * b + 256, :])
        for half in range(2):
            cols = pl.ds(half * HALF + 256 * b, 256)
            part = delta[64 * half:64 * half + 64, :]
            ua[:, cols] = part.astype(BF16)
            ur[:, cols] = (ug[:, cols].astype(F32) + ue[:, cols]) - part
    for b in range(DN_C // 256):
        cols = pl.ds(256 * b, 256)
        delta = nt3(wd[...], fd[256 * b:256 * b + 256, :])
        da[:, cols] = delta.astype(BF16)
        dr[:, cols] = (dg[:, cols].astype(F32) + de[:, cols]) - delta


def body(up_grad, up_error, up_warm, down_grad, down_error, down_warm):
    ug, ue, dg, de = up_grad[0], up_error[0], down_grad[0], down_error[0]
    vm = pl.BlockSpec(memory_space=pltpu.VMEM)
    hbm = pl.BlockSpec(memory_space=pl.ANY)
    dma = pltpu.SemaphoreType.DMA
    V = pltpu.VMEM
    f, wu, wd = pl.pallas_call(
        exchange,
        out_shape=(
            jax.ShapeDtypeStruct((NC, NX, NY, FR, 128), F32),
            jax.ShapeDtypeStruct((128, 128), F32),
            jax.ShapeDtypeStruct((128, 128), F32),
        ),
        in_specs=[hbm] * 6,
        out_specs=(hbm, vm, vm),
        scratch_shapes=[
            V((UP_R, UP_C), BF16), V((UP_R, UP_C), F32), V((RANK, UP_C), F32),
            V((DN_R, DN_C), BF16), V((DN_R, DN_C), F32), V((RANK, DN_C), F32),
            V((NC, NX, NY, SH, 128), F32), V((NX, NY, SH, 128), F32), V((NX - 1, NY, SH, 128), F32),
            V((NY - 1, SH, 128), F32), V((NC, NX, NY, FR, 128), F32),
            V((64, 128), F32), V((32, 128), F32), V((32, 128), F32), V((3, 8, 128), F32),
            V((NZ, 8, 128), F32), V((NY, 8, 128), F32), V((2, 32, 128), F32),
            dma((6,)), dma((4,)), dma((4,)), dma((3,)), dma((3,)), dma((7,)), dma((7,)),
            dma, dma, dma((3,)), dma((3,)), dma((7,)), dma((7,)), dma((7,)), dma((7,)), dma((3,)), dma((3,)), dma, dma,
            dma((7,)), dma((7,)), dma((3,)), dma((3,)), dma((4,)), dma((4,)), dma,
        ],
        compiler_params=pltpu.CompilerParams(
            collective_id=0, has_side_effects=True, vmem_limit_bytes=32 * 1024 * 1024),
        name="exchange",
    )(ug, ue, up_warm.T, dg, de, down_warm.T)
    ua, ur, da, dr = pl.pallas_call(
        finish,
        out_shape=(
            jax.ShapeDtypeStruct((UP_R, UP_C), BF16),
            jax.ShapeDtypeStruct((UP_R, UP_C), F32),
            jax.ShapeDtypeStruct((DN_R, DN_C), BF16),
            jax.ShapeDtypeStruct((DN_R, DN_C), F32),
        ),
        in_specs=[vm] * 7,
        out_specs=(vm,) * 4,
        scratch_shapes=[V((HALF, 128), F32), V((DN_C, 128), F32)],
        compiler_params=pltpu.CompilerParams(vmem_limit_bytes=32 * 1024 * 1024),
        name="finish",
    )(f, wu, wd, ug, ue, dg, de)
    return ua, ur[None], da, dr[None]


def solution(mesh):
    return jax.shard_map(
        body,
        mesh=mesh,
        in_specs=(
            P("dp", None, "mp"),
            P("dp", None, "mp"),
            P("mp", None),
            P("dp", None, "mp"),
            P("dp", None, "mp"),
            P("mp", None),
        ),
        out_specs=(P(None, "mp"), P("dp", None, "mp"), P(None, "mp"), P("dp", None, "mp")),
        check_vma=False,
    )
```

time: 515 us -> 56.6 us (0.11)
  blocking collectives: 279 us -> 0 us
  waiting for transfers between devices: 194 us -> 0 us
  Pallas kernels: 0 us -> 49.5 us
  between operations: 14.2 us -> 0.66 us
  other arithmetic: 13.4 us -> 0 us
  matrix products: 11.4 us -> 0 us
    psum x2 -> x0, blocking collectives: 279 us -> none  [the longest x1 249 us: body(): up_proj, down_proj = lax.psum((up_proj, down_proj), 'dp')]
    psum x1 -> x0, waiting for transfers between devices: 194 us -> none  [body(): up_total, down_total = lax.psum((up_back, down_back), 'dp')]
    pallas_call x0 -> x2, Pallas kernels: none -> 49.5 us  [the longest x1 47.6 us: body(): pl.pallas_call(exchange, out_shape=(jax.ShapeDtypeStruct((NC, NX, NY, FR,...]
    another operation x10 -> x0, other arithmetic: 13.4 us -> none  [the longest x6 7.2 us: orthonormal(): chol = jnp.linalg.cholesky(gram)]
    dot_general x8 -> x0, matrix products: 11 us -> none  [the longest x2 4.66 us: expand(): lax.dot_general(ortho, factor, (((1,), (1,)), ((), ())), precision=lax.Pr...]
  transfers between devices with their start and end apart: 1 -> 0, of which waited for: 1 -> 0; matrix products, arithmetic and copies ran while one was open for 0% -> 0% of each run, Pallas kernels for 0% -> 0%
where the time goes in v1:
time: 56.6 us; the launch traced here: 56.2 us
  Pallas kernels  49.5 us (87%)
  local copies, waits for them, and re-layouts  6.11 us (11%)
  between operations  0.66 us (1%)
    pallas_call x1, Pallas kernels, body(): pl.pallas_call(exchange, out_shape=(jax.ShapeDtypeStruct((NC, NX, NY, FR,...  47.6 us
    unnamed x14, local copies, waits for them, and re-layouts  6.11 us
    pallas_call x1, Pallas kernels, body(): pl.pallas_call(finish, out_shape=(jax.ShapeDtypeStruct((UP_R, UP_C), BF16...  1.89 us

profile of v1, /device:TPU:1, one launch (start us, length us, event | category | flops | bytes accessed | tf_op | source)
XLA Modules:
  0.0 56.2 jit_solution(8586520822934513965)
XLA Ops:
  0.6 0.0 copy-start
  0.6 1.2 %copy-done = f32[1,64,3584]{2,1,0:T(8,128)S(1)} copy-done((f32[1,64,3584]{2,1,0:T(8,128)S(1)}, f32[1,64,3584]{2,1,0:T(8,128)}, u32[]{:S(2)}) %copy-start) | copy-done | bytes 917528
  1.8 0.0 copy-start.1
  1.8 1.0 %copy-done.1 = f32[1,128,1024]{2,1,0:T(8,128)S(1)} copy-done((f32[1,128,1024]{2,1,0:T(8,128)S(1)}, f32[1,128,1024]{2,1,0:T(8,128)}, u32[]{:S(2)}) %copy-start.1) | copy-done | bytes 524312
  2.9 0.0 copy-start.3
  2.9 1.0 %copy-done.3 = bf16[1,64,3584]{2,1,0:T(8,128)(2,1)S(1)} copy-done((bf16[1,64,3584]{2,1,0:T(8,128)(2,1)S(1)}, bf16[1,64,3584]{2,1,0:T(8,128)(2,1)}, u32[]{:S(2)}) %copy-start.3) | copy-done | bytes 458776
  3.9 0.0 copy-start.4
  3.9 0.9 %copy-done.4 = bf16[1,128,1024]{2,1,0:T(8,128)(2,1)S(1)} copy-done((bf16[1,128,1024]{2,1,0:T(8,128)(2,1)S(1)}, bf16[1,128,1024]{2,1,0:T(8,128)(2,1)}, u32[]{:S(2)}) %copy-start.4) | copy-done | bytes 262168
  4.8 0.0 copy-start.5
  4.8 1.0 %copy-done.5 = f32[3584,32]{0,1:T(8,128)S(1)} copy-done((f32[3584,32]{0,1:T(8,128)S(1)}, f32[3584,32]{0,1:T(8,128)}, u32[]{:S(2)}) %copy-start.5) | copy-done | bytes 458776
  5.8 0.0 copy-start.6
  5.8 0.9 %copy-done.6 = f32[1024,32]{0,1:T(8,128)S(1)} copy-done((f32[1024,32]{0,1:T(8,128)S(1)}, f32[1024,32]{0,1:T(8,128)}, u32[]{:S(2)}) %copy-start.6) | copy-done | bytes 131096
  6.7 0.0 copy-start.2
  6.8 47.6 %exchange.1 = (f32[2,4,8,24,128]{4,3,2,1,0:T(8,128)S(1)}, f32[128,128]{1,0:T(8,128)S(1)}, f32[128,128]{1,0:T(8,128)S(1)}) custom-call(bf16[64,3584]{1,0:T(8,128)(2,1)S(1)} %bitcast.12, f32[64,3584]{1,0:T(8,128)S(1)} %bitcast.8, f32[32,3584]{1,0:T(8,128)S(1)} %bitcast.16, bf16[128,1024]{1,0:T(8,128)(2,1)S(1)} %bitcast.14, f32[128,1024]{1,0:T(8,128)S(1)} %bitcast.10, ...), custom_call_target="tpu_custom_call" | custom-call | tf_op jit(solution)/shard_map/exchange/pallas_call | solution.py:282
  54.3 0.0 copy-done.2
  54.3 1.9 %finish.1 = (bf16[64,3584]{1,0:T(8,128)(2,1)}, f32[64,3584]{1,0:T(8,128)}, bf16[128,1024]{1,0:T(8,128)(2,1)}, f32[128,1024]{1,0:T(8,128)}) custom-call(f32[2,4,8,24,128]{4,3,2,1,0:T(8,128)S(1)} %get-tuple-element.11.f, f32[128,128]{1,0:T(8,128)S(1)} %get-tuple-element.12.wu, f32[128,128]{1,0:T(8,128)S(1)} %get-tuple-element.13.wd, ...), custom_call_target="tpu_custom_call" | custom-call | tf_op jit(solution)/shard_map/finish/pallas_call | solution.py:306
Async XLA Ops:
  0.6 1.2 %copy-start = (f32[1,64,3584]{2,1,0:T(8,128)S(1)}, f32[1,64,3584]{2,1,0:T(8,128)}, u32[]{:S(2)}) copy-start(f32[1,64,3584]{2,1,0:T(8,128)} %param.7) | copy-start | bytes 2752516
  1.8 1.0 %copy-start.1 = (f32[1,128,1024]{2,1,0:T(8,128)S(1)}, f32[1,128,1024]{2,1,0:T(8,128)}, u32[]{:S(2)}) copy-start(f32[1,128,1024]{2,1,0:T(8,128)} %param.10) | copy-start | bytes 1572868
  2.9 1.0 %copy-start.3 = (bf16[1,64,3584]{2,1,0:T(8,128)(2,1)S(1)}, bf16[1,64,3584]{2,1,0:T(8,128)(2,1)}, u32[]{:S(2)}) copy-start(bf16[1,64,3584]{2,1,0:T(8,128)(2,1)} %param.6) | copy-start | bytes 1376260
  3.9 0.9 %copy-start.4 = (bf16[1,128,1024]{2,1,0:T(8,128)(2,1)S(1)}, bf16[1,128,1024]{2,1,0:T(8,128)(2,1)}, u32[]{:S(2)}) copy-start(bf16[1,128,1024]{2,1,0:T(8,128)(2,1)} %param.9) | copy-start | bytes 786436
  4.8 1.0 %copy-start.5 = (f32[3584,32]{0,1:T(8,128)S(1)}, f32[3584,32]{0,1:T(8,128)}, u32[]{:S(2)}) copy-start(f32[3584,32]{0,1:T(8,128)} %param.8) | copy-start | bytes 1376260
  5.8 0.9 %copy-start.6 = (f32[1024,32]{0,1:T(8,128)S(1)}, f32[1024,32]{0,1:T(8,128)}, u32[]{:S(2)}) copy-start(f32[1024,32]{0,1:T(8,128)} %param.11) | copy-start | bytes 393220
  6.7 47.6 %copy-start.2 = (f32[1,128,1024]{2,1,0:T(8,128)S(1)}, f32[1,128,1024]{2,1,0:T(8,128)}, u32[]{:S(2)}) copy-start(f32[1,128,1024]{2,1,0:T(8,128)} %param.10) | copy-start | bytes 1572868

commit v2 on v1

v2 whole, which is shorter than its diff:
```python
import jax
import jax.numpy as jnp
from jax import lax
from jax.experimental import pallas as pl
from jax.experimental.pallas import tpu as pltpu
from jax.sharding import PartitionSpec as P

F32 = jnp.float32
BF16 = jnp.bfloat16
HI = lax.Precision.HIGHEST
MESH = pl.DeviceIdType.MESH
NY, NX, NC, NZ = 8, 4, 2, 8
RANK = 32
UP_R, UP_C = 64, 3584
DN_R, DN_C = 128, 1024
HALF = UP_C // 2


def nt(a, b, precision=None):
    return lax.dot_general(a, b, (((1,), (1,)), ((), ())), preferred_element_type=F32, precision=precision)


def split(a):
    hi = a.astype(BF16)
    return hi, (a - hi.astype(F32)).astype(BF16)


def nt3(a, b):
    ah, al = split(a)
    bh, bl = split(b)
    return nt(ah, bh) + nt(ah, bl) + nt(al, bh)


def eliminate(a1, a2):
    shape = (RANK, 128)
    row = lax.broadcasted_iota(jnp.int32, shape, 0)
    lane = lax.broadcasted_iota(jnp.int32, shape, 1)
    in_dn = lane >= 96
    scale_u = jnp.ones(shape, F32)
    scale_d = jnp.ones(shape, F32)
    for panel in range(4):
        first = panel * 8
        cu = [jnp.broadcast_to(a1[:, 64 + first + m:65 + first + m], shape) for m in range(8)]
        cd = [jnp.broadcast_to(a1[:, 96 + first + m:97 + first + m], shape) for m in range(8)]
        for m in range(8):
            k = first + m
            below = row > k
            pu = cu[m][k:k + 1, :]
            pd = cd[m][k:k + 1, :]
            fu = jnp.where(below, cu[m] * (1.0 / pu), 0.0)
            fd = jnp.where(below, cd[m] * (1.0 / pd), 0.0)
            for n in range(m + 1, 8):
                cu[n] = cu[n] - fu * cu[n][k:k + 1, :]
                cd[n] = cd[n] - fd * cd[n][k:k + 1, :]
            a1 = a1 - jnp.where(in_dn, fd, fu) * a1[k:k + 1, :]
            a2 = a2 - fd * a2[k:k + 1, :]
            scale_u = jnp.where(row == k, lax.rsqrt(pu), scale_u)
            scale_d = jnp.where(row == k, lax.rsqrt(pd), scale_d)
    return a1 * scale_u, a2 * scale_d


def exchange(ug, ue, uw, dg, de, dw, fa_out, fb_out, wu_out, wd_out,
             vug, vue, vuw, vdg, vde, vdw, TU, TD, CU, CD, XU, YD, YU, XD, FA, FB,
             pt, pc, px, pxr, pz, py, pg,
             in_sem, s_cu, r_cu, s_cd, r_cd, s_xu, r_xu, s_yd, r_yd, s_yu, r_yu, s_xd, r_xd,
             s_pc, r_pc, s_px, r_px, s_pz, r_pz, s_py, r_py, s_pa, r_pa, s_pb, r_pb,
             s_ay, r_ay, s_ax, r_ax, s_ac, r_ac, s_bx, r_bx, s_by, r_by, s_bc, r_bc, out_sem):
    d = lax.axis_index("dp")
    z = lax.axis_index("mp")
    c = lax.rem(d, 2)
    x = lax.rem(lax.div(d, 2), NX)
    y = lax.div(d, 8)
    other = 1 - c

    def at(yy, xx, cc):
        return ((yy * NX + xx) * NC + cc, z)

    partner = at(y, x, other)

    def xpeer(o):
        return at(y, lax.rem(x + o, NX), c)

    def ypeer(o):
        return at(lax.rem(y + o, NY), x, c)

    def zpeer(o):
        return (d, lax.rem(z + o, NZ))

    bar = pltpu.get_barrier_semaphore()
    for o in (4, 3, 5, 2, 6, 1, 7):
        pl.semaphore_signal(bar, 1, device_id=zpeer(o), device_id_type=MESH)
        pl.semaphore_signal(bar, 1, device_id=ypeer(o), device_id_type=MESH)
    for o in (2, 1, 3):
        pl.semaphore_signal(bar, 1, device_id=xpeer(o), device_id_type=MESH)
    pl.semaphore_signal(bar, 1, device_id=partner, device_id_type=MESH)

    loads = [pltpu.make_async_copy(a, b, in_sem.at[i])
             for i, (a, b) in enumerate([(dg, vdg), (de, vde), (dw, vdw), (ug, vug), (ue, vue), (uw, vuw)])]
    for cp in loads:
        cp.start()

    def down_part(b):
        cols = pl.ds(256 * b, 256)
        return vdg[:, cols].astype(F32) + vde[:, cols]

    def up_part(half, b):
        cols = pl.ds(half * HALF + 256 * b, 256)
        return vug[:, cols].astype(F32) + vue[:, cols]

    for cp in loads[:3]:
        cp.wait()
    acc = jnp.zeros((RANK, DN_R), F32)
    for b in range(DN_C // 256):
        acc += nt3(vdw[:, pl.ds(256 * b, 256)], down_part(b))
    pt[32:64, :] = acc
    for cp in loads[3:]:
        cp.wait()
    acc = jnp.zeros((RANK, UP_R), F32)
    for b in range(HALF // 256):
        for half in range(2):
            acc += nt3(vuw[:, pl.ds(half * HALF + 256 * b, 256)], up_part(half, b))
    pt[0:32, :] = jnp.concatenate([acc, jnp.zeros((RANK, 64), F32)], axis=1)

    pl.semaphore_wait(bar, 1 + 7 + 7 + 3)

    sent = []

    def remote(src, dst, ssem, rsem, dev):
        cp = pltpu.make_async_remote_copy(src_ref=src, dst_ref=dst, send_sem=ssem, recv_sem=rsem,
                                          device_id=dev, device_id_type=MESH)
        cp.start()
        sent.append(cp)
        return cp

    cp_pc = remote(pt.at[pl.ds(pl.multiple_of(other * 32, 32), 32)], pc, s_pc, r_pc, partner)

    for b in range(HALF // 256):
        stacked = jnp.concatenate([up_part(0, b), up_part(1, b)], axis=0)
        for s in range(2):
            turned = stacked[:, 128 * s:128 * (s + 1)].T
            for i in range(16):
                tile = (2 * b + s) * 16 + i
                q, u = tile // 7, tile % 7
                rows = turned[8 * i:8 * i + 8, :]
                if u <= 3:
                    TU[0, q // NY, q % NY, 8 * u:8 * u + 8, :] = rows
                if u >= 3:
                    TU[1, q // NY, q % NY, 8 * (u - 3):8 * (u - 3) + 8, :] = rows

    cp_pc.wait_recv()
    px[...] = pt[pl.ds(pl.multiple_of(c * 32, 32), 32), :] + pc[...]
    cp_px = [remote(px.at[pl.ds(pl.multiple_of(lax.rem(x + o, NX) * 8, 8), 8)], pxr.at[o - 1],
                    s_px.at[o - 1], r_px.at[o - 1], xpeer(o)) for o in (2, 1, 3)]

    for b in range(DN_C // 256):
        m = down_part(b)
        for s in range(2):
            turned = m[:, 128 * s:128 * (s + 1)].T
            for i in range(16):
                tile = (2 * b + s) * 16 + i
                q, u = tile // 4, tile % 4
                TD[u // 2, q % NY, q // NY, 8 * (u % 2):8 * (u % 2) + 8, :] = turned[8 * i:8 * i + 8, :]

    order = [(0, 2), (1, 4), (1, 3), (1, 5), (0, 1), (1, 2), (1, 6), (0, 3), (1, 1), (1, 7), (0, 0), (1, 0)]
    cp_c = {}
    for kind, o in order:
        if kind == 0:
            xx = lax.rem(x + o, NX)
            cp_c[kind, o] = remote(TU.at[other, xx], CU.at[xx], s_cu.at[o], r_cu.at[o], partner)
        else:
            yy = lax.rem(y + o, NY)
            cp_c[kind, o] = remote(TD.at[other, yy], CD.at[yy], s_cd.at[o], r_cd.at[o], partner)
    cp_xu, cp_yd = [], []
    for kind, o in order:
        cp_c[kind, o].wait_recv()
        if kind == 0:
            xx = lax.rem(x + o, NX)
            TU[c, xx] = TU[c, xx] + CU[xx]
            if o:
                cp_xu.append(remote(TU.at[c, xx], XU.at[o - 1], s_xu.at[o - 1], r_xu.at[o - 1], xpeer(o)))
        else:
            yy = lax.rem(y + o, NY)
            TD[c, yy] = TD[c, yy] + CD[yy]
            if o:
                cp_yd.append(remote(TD.at[c, yy], YD.at[o - 1], s_yd.at[o - 1], r_yd.at[o - 1], ypeer(o)))

    for cp in cp_px:
        cp.wait_recv()
    mine = pl.ds(pl.multiple_of(x * 8, 8), 8)
    pz[z] = (px[mine, :] + pxr[0]) + (pxr[1] + pxr[2])
    cp_pz = [remote(pz.at[z], pz.at[z], s_pz.at[o - 1], r_pz.at[o - 1], zpeer(o)) for o in (4, 3, 5, 2, 6, 1, 7)]
    for cp in cp_pz:
        cp.wait_recv()
    py[y] = ((pz[0] + pz[1]) + (pz[2] + pz[3])) + ((pz[4] + pz[5]) + (pz[6] + pz[7]))
    cp_py = [remote(py.at[y], py.at[y], s_py.at[o - 1], r_py.at[o - 1], ypeer(o)) for o in (4, 3, 5, 2, 6, 1, 7)]

    for cp in cp_xu:
        cp.wait_recv()
    cp_yu = []
    for o in (4, 3, 5, 2, 6, 1, 7, 0):
        yy = lax.rem(y + o, NY)
        TU[c, x, yy] = (TU[c, x, yy] + XU[0, yy]) + (XU[1, yy] + XU[2, yy])
        if o:
            cp_yu.append(remote(TU.at[c, x, yy], YU.at[o - 1], s_yu.at[o - 1], r_yu.at[o - 1], ypeer(o)))

    for cp in cp_py:
        cp.wait_recv()
    pg[c, mine, :] = ((py[0] + py[1]) + (py[2] + py[3])) + ((py[4] + py[5]) + (py[6] + py[7]))
    cp_pa = [remote(pg.at[c, mine], pg.at[c, mine], s_pa.at[o - 1], r_pa.at[o - 1], xpeer(o)) for o in (2, 1, 3)]

    for cp in cp_yd:
        cp.wait_recv()
    cp_xd = []
    for o in (2, 1, 3, 0):
        xx = lax.rem(x + o, NX)
        tot = TD[c, y, xx]
        for i in range(NY - 1):
            tot = tot + YD[i, xx]
        TD[c, y, xx] = tot
        if o:
            cp_xd.append(remote(TD.at[c, y, xx], XD.at[o - 1], s_xd.at[o - 1], r_xd.at[o - 1], xpeer(o)))

    for cp in cp_pa:
        cp.wait_recv()
    cp_pb = remote(pg.at[c], pg.at[c], s_pb, r_pb, partner)
    cp_pb.wait_recv()

    a1 = pg[0]
    a2 = pg[1]
    gu = nt(a1, a1, HI)
    gd = nt(a2, a2, HI)
    a1, a2 = eliminate(jnp.concatenate([a1[:, :64], gu, gd], axis=1), a2)
    lane = lax.broadcasted_iota(jnp.int32, (RANK, 128), 1)
    left = jnp.where(lane < 64, a1, 0.0)
    right = pltpu.roll(left, 64, axis=1)
    wu = jnp.concatenate([left, right, left, right], axis=0)
    wd = jnp.concatenate([a2, a2, a2, a2], axis=0)

    lane16 = lax.broadcasted_iota(jnp.int32, (16, 128), 1)
    for cp in cp_xd:
        cp.wait_recv()
    shard = ((TD[c, y, x] + XD[0]) + (XD[1] + XD[2])) * (1.0 / 64.0)
    rd = nt(shard, wd, HI)
    FB[c, y, x] = jnp.where(lane16[0:8] < 32, rd[0:8], rd[8:16])
    cp_bx = [remote(FB.at[c, y, x], FB.at[c, y, x], s_bx.at[o - 1], r_bx.at[o - 1], xpeer(o)) for o in (2, 1, 3)]
    for cp in cp_yu:
        cp.wait_recv()
    shard = TU[c, x, y]
    for i in range(NY - 1):
        shard = shard + YU[i]
    ru = nt(shard * (1.0 / 64.0), wu, HI)
    FA[c, x, y] = jnp.where(lane16 < 64, ru[0:16], ru[16:32])
    cp_ay = [remote(FA.at[c, x, y], FA.at[c, x, y], s_ay.at[o - 1], r_ay.at[o - 1], ypeer(o)) for o in (4, 3, 5, 2, 6, 1, 7)]
    wu_out[...] = wu.T
    wd_out[...] = wd.T
    for cp in cp_bx:
        cp.wait_recv()
    yo = (4, 3, 5, 2, 6, 1, 7)
    cp_by = [remote(FB.at[c, y], FB.at[c, y], s_by.at[o - 1], r_by.at[o - 1], ypeer(o)) for o in yo]
    cp_bc = [remote(FB.at[c, y], FB.at[c, y], s_bc.at[0], r_bc.at[0], partner)]
    for cp in cp_ay:
        cp.wait_recv()
    cp_ax = [remote(FA.at[c, x], FA.at[c, x], s_ax.at[o - 1], r_ax.at[o - 1], xpeer(o)) for o in (2, 1, 3)]
    cp_ac = [remote(FA.at[c, x], FA.at[c, x], s_ac.at[0], r_ac.at[0], partner)]
    for cp, o in zip(cp_by, yo):
        cp.wait_recv()
        yy = lax.rem(y - o + NY, NY)
        cp_bc.append(remote(FB.at[c, yy], FB.at[c, yy], s_bc.at[o], r_bc.at[o], partner))
    for cp, o in zip(cp_ax, (2, 1, 3)):
        cp.wait_recv()
        xx = lax.rem(x - o + NX, NX)
        cp_ac.append(remote(FA.at[c, xx], FA.at[c, xx], s_ac.at[o], r_ac.at[o], partner))
    outs = [pltpu.make_async_copy(FA.at[c], fa_out.at[c], out_sem.at[0]),
            pltpu.make_async_copy(FB.at[c], fb_out.at[c], out_sem.at[1])]
    for cp in outs:
        cp.start()
    for cp in cp_bc:
        cp.wait_recv()
    outs.append(pltpu.make_async_copy(FB.at[other], fb_out.at[other], out_sem.at[3]))
    outs[-1].start()
    for cp in cp_ac:
        cp.wait_recv()
    outs.append(pltpu.make_async_copy(FA.at[other], fa_out.at[other], out_sem.at[2]))
    outs[-1].start()
    for cp in sent:
        cp.wait_send()
    for cp in outs:
        cp.wait()


def finish(fa, fb, wu, wd, ug, ue, dg, de, ua, ur, da, dr, fu, fd):
    lane = lax.broadcasted_iota(jnp.int32, (8, 128), 1)
    for tile in range(HALF // 8):
        q, u = tile // 7, tile % 7
        core, s = (0, u) if u <= 3 else (1, u - 3)
        r0 = (s % 2) * 8
        rows = fa[core, q // NY, q % NY, r0:r0 + 8, :]
        fu[8 * tile:8 * tile + 8, :] = jnp.where(lane // 64 == s // 2, rows, 0.0)
    for tile in range(DN_C // 8):
        q, u = tile // 4, tile % 4
        rows = fb[u // 2, q % NY, q // NY]
        fd[8 * tile:8 * tile + 8, :] = jnp.where(lane // 32 == u % 2, rows, 0.0)
    for b in range(HALF // 256):
        delta = nt3(wu[...], fu[256 * b:256 * b + 256, :])
        for half in range(2):
            cols = pl.ds(half * HALF + 256 * b, 256)
            part = delta[64 * half:64 * half + 64, :]
            ua[:, cols] = part.astype(BF16)
            ur[:, cols] = (ug[:, cols].astype(F32) + ue[:, cols]) - part
    for b in range(DN_C // 256):
        cols = pl.ds(256 * b, 256)
        delta = nt3(wd[...], fd[256 * b:256 * b + 256, :])
        da[:, cols] = delta.astype(BF16)
        dr[:, cols] = (dg[:, cols].astype(F32) + de[:, cols]) - delta


def body(up_grad, up_error, up_warm, down_grad, down_error, down_warm):
    ug, ue, dg, de = up_grad[0], up_error[0], down_grad[0], down_error[0]
    vm = pl.BlockSpec(memory_space=pltpu.VMEM)
    hbm = pl.BlockSpec(memory_space=pltpu.HBM)
    dma = pltpu.SemaphoreType.DMA
    V = pltpu.VMEM
    fa, fb, wu, wd = pl.pallas_call(
        exchange,
        out_shape=(
            jax.ShapeDtypeStruct((NC, NX, NY, 16, 128), F32),
            jax.ShapeDtypeStruct((NC, NY, NX, 8, 128), F32),
            jax.ShapeDtypeStruct((128, 128), F32),
            jax.ShapeDtypeStruct((128, 128), F32),
        ),
        in_specs=[hbm] * 6,
        out_specs=(pl.BlockSpec(memory_space=pl.ANY),) * 2 + (vm, vm),
        scratch_shapes=[
            V((UP_R, UP_C), BF16), V((UP_R, UP_C), F32), V((RANK, UP_C), F32),
            V((DN_R, DN_C), BF16), V((DN_R, DN_C), F32), V((RANK, DN_C), F32),
            V((NC, NX, NY, 32, 128), F32), V((NC, NY, NX, 16, 128), F32),
            V((NX, NY, 32, 128), F32), V((NY, NX, 16, 128), F32),
            V((NX - 1, NY, 32, 128), F32), V((NY - 1, NX, 16, 128), F32),
            V((NY - 1, 32, 128), F32), V((NX - 1, 16, 128), F32),
            V((NC, NX, NY, 16, 128), F32), V((NC, NY, NX, 8, 128), F32),
            V((64, 128), F32), V((32, 128), F32), V((32, 128), F32), V((3, 8, 128), F32),
            V((NZ, 8, 128), F32), V((NY, 8, 128), F32), V((2, 32, 128), F32),
            dma((6,)), *[dma((n,)) for n in (4, 4, 8, 8, 3, 3, 7, 7, 7, 7, 3, 3)],
            dma, dma, dma((3,)), dma((3,)), dma((7,)), dma((7,)), dma((7,)), dma((7,)), dma((3,)), dma((3,)), dma, dma,
            *[dma((n,)) for n in (7, 7, 3, 3, 4, 4, 3, 3, 7, 7, 8, 8)], dma((4,)),
        ],
        compiler_params=pltpu.CompilerParams(
            collective_id=0, has_side_effects=True, vmem_limit_bytes=32 * 1024 * 1024),
        name="exchange",
    )(*[pltpu.with_memory_space_constraint(a, pltpu.HBM) for a in (ug, ue, up_warm.T, dg, de, down_warm.T)])
    ua, ur, da, dr = pl.pallas_call(
        finish,
        out_shape=(
            jax.ShapeDtypeStruct((UP_R, UP_C), BF16),
            jax.ShapeDtypeStruct((UP_R, UP_C), F32),
            jax.ShapeDtypeStruct((DN_R, DN_C), BF16),
            jax.ShapeDtypeStruct((DN_R, DN_C), F32),
        ),
        in_specs=[vm] * 8,
        out_specs=(vm,) * 4,
        scratch_shapes=[V((HALF, 128), F32), V((DN_C, 128), F32)],
        compiler_params=pltpu.CompilerParams(vmem_limit_bytes=32 * 1024 * 1024),
        name="finish",
    )(fa, fb, wu, wd, ug, ue, dg, de)
    return ua, ur[None], da, dr[None]


def solution(mesh):
    return jax.shard_map(
        body,
        mesh=mesh,
        in_specs=(
            P("dp", None, "mp"),
            P("dp", None, "mp"),
            P("mp", None),
            P("dp", None, "mp"),
            P("dp", None, "mp"),
            P("mp", None),
        ),
        out_specs=(P(None, "mp"), P("dp", None, "mp"), P(None, "mp"), P("dp", None, "mp")),
        check_vma=False,
    )
```

time: 56.6 us -> 49.4 us (0.87)
  local copies, waits for them, and re-layouts: 6.11 us -> 0.02 us
  Pallas kernels: 49.5 us -> 48.6 us
    unnamed x14 -> x8, local copies, waits for them, and re-layouts: 6.11 us -> 0.02 us
    pallas_call x1, Pallas kernels: 47.6 us -> 46.7 us  [body(): pl.pallas_call(exchange, out_shape=(jax.ShapeDtypeStruct((NC, NX, NY, 16,...]
where the time goes in v2:
time: 49.4 us; the launch traced here: 49.3 us
  Pallas kernels  48.6 us (98%)
  between operations  0.7 us (1%)
    pallas_call x1, Pallas kernels, body(): pl.pallas_call(exchange, out_shape=(jax.ShapeDtypeStruct((NC, NX, NY, 16,...  46.7 us
    pallas_call x1, Pallas kernels, body(): pl.pallas_call(finish, out_shape=(jax.ShapeDtypeStruct((UP_R, UP_C), BF16...  1.89 us

profile of v2, /device:TPU:1, one launch (start us, length us, event | category | flops | bytes accessed | tf_op | source)
XLA Modules:
  0.0 49.3 jit_solution(7644223781952893814)
XLA Ops:
  0.6 0.0 copy-start
  0.6 0.0 copy-start.1
  0.7 0.0 copy-start.2
  0.7 0.0 copy-start.3
  0.7 46.7 %exchange.1 = (f32[2,4,8,16,128]{4,3,2,1,0:T(8,128)S(1)}, f32[2,8,4,8,128]{4,3,2,1,0:T(8,128)S(1)}, f32[128,128]{1,0:T(8,128)S(1)}, f32[128,128]{1,0:T(8,128)S(1)}) custom-call(bf16[64,3584]{1,0:T(8,128)(2,1)} %bitcast.12, f32[64,3584]{1,0:T(8,128)} %bitcast.8, f32[32,3584]{1,0:T(8,128)} %bitcast.16, bf16[128,1024]{1,0:T(8,128)(2,1)} %bitcast.14, ...), custom_call_target="tpu_custom_call" | custom-call | tf_op jit(solution)/shard_map/exchange/pallas_call | solution.py:323
  47.4 0.0 copy-done
  47.4 0.0 copy-done.1
  47.4 0.0 copy-done.2
  47.4 0.0 copy-done.3
  47.4 1.9 %finish.1 = (bf16[64,3584]{1,0:T(8,128)(2,1)}, f32[64,3584]{1,0:T(8,128)}, bf16[128,1024]{1,0:T(8,128)(2,1)}, f32[128,1024]{1,0:T(8,128)}) custom-call(f32[2,4,8,16,128]{4,3,2,1,0:T(8,128)S(1)} %get-tuple-element.12.fa, f32[2,8,4,8,128]{4,3,2,1,0:T(8,128)S(1)} %get-tuple-element.13.fb, f32[128,128]{1,0:T(8,128)S(1)} %get-tuple-element.14.wu, ...), custom_call_target="tpu_custom_call" | custom-call | tf_op jit(solution)/shard_map/finish/pallas_call | solution.py:351
Async XLA Ops:
  0.6 46.7 %copy-start = (f32[1,64,3584]{2,1,0:T(8,128)S(1)}, f32[1,64,3584]{2,1,0:T(8,128)}, u32[]{:S(2)}) copy-start(f32[1,64,3584]{2,1,0:T(8,128)} %param.7) | copy-start | bytes 2752516
  0.6 46.7 %copy-start.1 = (f32[1,128,1024]{2,1,0:T(8,128)S(1)}, f32[1,128,1024]{2,1,0:T(8,128)}, u32[]{:S(2)}) copy-start(f32[1,128,1024]{2,1,0:T(8,128)} %param.10) | copy-start | bytes 1572868
  0.7 46.7 %copy-start.2 = (bf16[1,64,3584]{2,1,0:T(8,128)(2,1)S(1)}, bf16[1,64,3584]{2,1,0:T(8,128)(2,1)}, u32[]{:S(2)}) copy-start(bf16[1,64,3584]{2,1,0:T(8,128)(2,1)} %param.6) | copy-start | bytes 1376260
  0.7 46.7 %copy-start.3 = (bf16[1,128,1024]{2,1,0:T(8,128)(2,1)S(1)}, bf16[1,128,1024]{2,1,0:T(8,128)(2,1)}, u32[]{:S(2)}) copy-start(bf16[1,128,1024]{2,1,0:T(8,128)(2,1)} %param.9) | copy-start | bytes 786436

commit v3 on v0

v3 whole, which is shorter than its diff:
```python
import jax
import jax.numpy as jnp
from jax import lax
from jax.experimental import pallas as pl
from jax.experimental.pallas import tpu as pltpu
from jax.sharding import PartitionSpec as P

F32 = jnp.float32
BF16 = jnp.bfloat16
HI = lax.Precision.HIGHEST
MESH = pl.DeviceIdType.MESH
NY, NX, NC, NZ = 8, 4, 2, 8
RANK = 32
UP_R, UP_C = 64, 3584
DN_R, DN_C = 128, 1024
HALF = UP_C // 2


def nt(a, b, precision=None):
    return lax.dot_general(a, b, (((1,), (1,)), ((), ())), preferred_element_type=F32, precision=precision)


def split(a):
    hi = a.astype(BF16)
    return hi, (a - hi.astype(F32)).astype(BF16)


def nt3(a, b):
    ah, al = split(a)
    bh, bl = split(b)
    return nt(ah, bh) + nt(ah, bl) + nt(al, bh)


def eliminate(arrays, where, off):
    shape = (RANK, 128)
    row = lax.broadcasted_iota(jnp.int32, shape, 0)
    scale = jnp.ones(shape, F32)
    for first in range(0, RANK, 8):
        cols = [jnp.broadcast_to(arrays[where][:, off + first + m:off + first + m + 1], shape) for m in range(8)]
        for m in range(8):
            k = first + m
            pivot = cols[m][k:k + 1, :]
            factor = jnp.where(row > k, cols[m] * (1.0 / pivot), 0.0)
            for n in range(m + 1, 8):
                cols[n] = cols[n] - factor * cols[n][k:k + 1, :]
            arrays = [a - factor * a[k:k + 1, :] for a in arrays]
            scale = jnp.where(row == k, lax.rsqrt(pivot), scale)
    return arrays[0] * scale


def exchange(ug, ue, uw, dg, de, dw, FA0, FA1, FB, wu_out, wd_out,
             vug, vue, vuw, vdg, vde, vdw, TU0, TU1, TD0, TD1, CU0, CU1, CD, XU0, XU1, YD, YU0, YU1, XD0, XD1,
             SA0, SA1, SB, SW, pt, pc, px, pxr, pz, py, pg,
             in_sem, s_cu, r_cu, s_cd, r_cd, s_xu, r_xu, s_yd, r_yd, s_yu, r_yu, s_xd, r_xd, s_vu, r_vu, s_vd, r_vd,
             s_px, r_px, s_pz, r_pz, s_py, r_py, s_pa, r_pa,
             s_ay, r_ay, s_a1, r_a1, s_ax, r_ax, s_ac, r_ac, s_ad, r_ad, s_bx, r_bx, s_by, r_by, s_bc, r_bc, own_sem,
             s_pc, r_pc, s_wu, r_wu, s_wd, r_wd):
    d = lax.axis_index("dp")
    z = lax.axis_index("mp")
    c = lax.rem(d, 2)
    x = lax.rem(lax.div(d, 2), NX)
    y = lax.div(d, 8)
    other = 1 - c
    far_y = (4, 3, 5, 2, 6, 1, 7)
    far_x = (2, 1, 3)

    def at(yy, xx, cc):
        return ((yy * NX + xx) * NC + cc, z)

    partner = at(y, x, other)

    xs = [lax.rem(x + o, NX) for o in range(NX)]
    ys = [lax.rem(y + o, NY) for o in range(NY)]
    zs = [lax.rem(z + o, NZ) for o in range(NZ)]

    def xof(o):
        return xs[o % NX]

    def yof(o):
        return ys[o % NY]

    def xpeer(o):
        return at(y, xof(o), c)

    def ypeer(o):
        return at(yof(o), x, c)

    def zpeer(o):
        return (d, zs[o])

    pairs = []
    for half in range(2):
        cols = pl.ds(half * HALF, HALF)
        pairs += [(ug.at[:, cols], vug.at[:, cols]), (ue.at[:, cols], vue.at[:, cols]), (uw.at[:, cols], vuw.at[:, cols])]
    pairs += [(dg, vdg), (de, vde), (dw, vdw)]
    loads = [pltpu.make_async_copy(a, b, in_sem.at[i]) for i, (a, b) in enumerate(pairs)]
    for cp in loads:
        cp.start()

    bar = pltpu.get_barrier_semaphore()
    for o in far_y:
        pl.semaphore_signal(bar, 1, device_id=zpeer(o), device_id_type=MESH)
        pl.semaphore_signal(bar, 1, device_id=ypeer(o), device_id_type=MESH)
    for o in far_x:
        pl.semaphore_signal(bar, 1, device_id=xpeer(o), device_id_type=MESH)
    pl.semaphore_signal(bar, 1, device_id=partner, device_id_type=MESH)

    def down_part(b):
        cols = pl.ds(256 * b, 256)
        return vdg[:, cols].astype(F32) + vde[:, cols]

    def up_part(half, b):
        cols = pl.ds(half * HALF + 256 * b, 256)
        return vug[:, cols].astype(F32) + vue[:, cols]

    acc = jnp.zeros((RANK, UP_R), F32)
    for half in range(2):
        for cp in loads[3 * half:3 * half + 3]:
            cp.wait()
        for b in range(HALF // 256):
            acc += nt3(vuw[:, pl.ds(half * HALF + 256 * b, 256)], up_part(half, b))
    pt[0:32, :] = jnp.concatenate([acc, jnp.zeros((RANK, 64), F32)], axis=1)
    for cp in loads[6:]:
        cp.wait()
    acc = jnp.zeros((RANK, DN_R), F32)
    for b in range(DN_C // 256):
        acc += nt3(vdw[:, pl.ds(256 * b, 256)], down_part(b))
    pt[32:64, :] = acc

    pl.semaphore_wait(bar, 1 + 7 + 7 + 3)

    def describe(src, dst, ssem, rsem, dev):
        return pltpu.make_async_remote_copy(src_ref=src, dst_ref=dst, send_sem=ssem, recv_sem=rsem,
                                            device_id=dev, device_id_type=MESH)

    def remote(log, src, dst, ssem, rsem, dev):
        cp = describe(src, dst, ssem, rsem, dev)
        cp.start()
        log.append(cp)
        return cp

    sent = []
    cp_pc = remote(sent, pt.at[pl.ds(pl.multiple_of(other * 32, 32), 32)], pc, s_pc, r_pc, partner)

    for b in range(HALF // 256):
        stacked = jnp.concatenate([up_part(0, b), up_part(1, b)], axis=0)
        for s in range(2):
            turned = stacked[:, 128 * s:128 * (s + 1)].T
            for i in range(16):
                tile = (2 * b + s) * 16 + i
                q, u = tile // 7, tile % 7
                dst, r0 = (TU0, 8 * u) if u < 4 else (TU1, 8 * u - 32)
                dst[q // NY, q % NY, r0:r0 + 8, :] = turned[8 * i:8 * i + 8, :]

    cp_pc.wait_recv()
    px[...] = pt[pl.ds(pl.multiple_of(c * 32, 32), 32), :] + pc[...]
    cp_px = [remote(sent, px.at[pl.ds(pl.multiple_of(xof(o) * 8, 8), 8)], pxr.at[o - 1],
                    s_px.at[o - 1], r_px.at[o - 1], xpeer(o)) for o in far_x]

    for b in range(DN_C // 256):
        m = down_part(b)
        for s in range(2):
            turned = m[:, 128 * s:128 * (s + 1)].T
            for i in range(4):
                q = (2 * b + s) * 4 + i
                TD0[q // NX, q % NX] = turned[32 * i:32 * i + 16, :]
                TD1[q // NX, q % NX] = turned[32 * i + 16:32 * i + 32, :]

    mine = pl.ds(pl.multiple_of(x * 8, 8), 8)

    def proj_z(log):
        for cp in cp_px:
            cp.wait_recv()
        pz[z] = (px[mine, :] + pxr[0]) + (pxr[1] + pxr[2])
        return [remote(log, pz.at[z], pz.at[z], s_pz.at[o - 1], r_pz.at[o - 1], zpeer(o)) for o in far_y]

    def proj_y(log, cps):
        for cp in cps:
            cp.wait_recv()
        py[y] = ((pz[0] + pz[1]) + (pz[2] + pz[3])) + ((pz[4] + pz[5]) + (pz[6] + pz[7]))
        return [remote(log, py.at[y], py.at[y], s_py.at[o - 1], r_py.at[o - 1], ypeer(o)) for o in far_y]

    def proj_x(log, cps):
        for cp in cps:
            cp.wait_recv()
        pg[mine, :] = ((py[0] + py[1]) + (py[2] + py[3])) + ((py[4] + py[5]) + (py[6] + py[7]))
        return [remote(log, pg.at[mine], pg.at[mine], s_pa.at[o - 1], r_pa.at[o - 1], xpeer(o)) for o in far_x]

    lane = lax.broadcasted_iota(jnp.int32, (RANK, 128), 1)
    lane16 = lane[0:16]
    lane8 = lane[0:8]

    def local(log, src, dst, sem):
        cp = pltpu.make_async_copy(src, dst, sem)
        cp.start()
        log.append(cp)
        return cp

    def sum_merged(core, log):
        tu, tu_other = (TU0, TU1) if core == 0 else (TU1, TU0)
        td, td_other = (TD0, TD1) if core == 0 else (TD1, TD0)
        cu, cu_other = (CU0, CU1) if core == 0 else (CU1, CU0)
        xu = XU0 if core == 0 else XU1
        order = [(0, 2), (1, 4), (1, 3), (1, 5), (0, 1), (1, 2), (1, 6), (0, 3), (1, 1), (1, 7), (0, 0), (1, 0)]
        for kind, o in order:
            if kind == 0:
                remote(log, tu_other.at[xs[o]], cu_other.at[xs[o]], s_cu.at[o], r_cu.at[o], partner)
            else:
                remote(log, td_other.at[ys[o]], CD.at[ys[o]], s_cd.at[o], r_cd.at[o], partner)
        cp_xu, cp_yd = [], []
        for kind, o in order:
            if kind == 0:
                xx = xs[o]
                describe(tu.at[xx], cu.at[xx], s_cu.at[o], r_cu.at[o], partner).wait_recv()
                tu[xx] = tu[xx] + cu[xx]
                if o:
                    cp_xu.append(remote(log, tu.at[xx], xu.at[o - 1], s_xu.at[o - 1], r_xu.at[o - 1], xpeer(o)))
            else:
                yy = ys[o]
                describe(td.at[yy], CD.at[yy], s_cd.at[o], r_cd.at[o], partner).wait_recv()
                td[yy] = td[yy] + CD[yy]
                if o:
                    cp_yd.append(remote(log, td.at[yy], YD.at[o - 1], s_yd.at[o - 1], r_yd.at[o - 1], ypeer(o)))

        cp_py = proj_y(log, proj_z(log))

        for cp in cp_xu:
            cp.wait_recv()
        for o in far_y + (0,):
            yy = ys[o]
            tu[x, yy] = (tu[x, yy] + xu[0, yy]) + (xu[1, yy] + xu[2, yy])
            if core == 1:
                remote(log, tu.at[x, yy], YU1.at[o], s_vu.at[o], r_vu.at[o], at(yy, x, 0))
            elif o:
                remote(log, tu.at[x, yy], YU0.at[o - 1], s_yu.at[o - 1], r_yu.at[o - 1], at(yy, x, 0))

        cp_pa = proj_x(log, cp_py)

        for cp in cp_yd:
            cp.wait_recv()
        for o in far_x + (0,):
            xx = xs[o]
            tot = td[y, xx]
            for i in range(NY - 1):
                tot = tot + YD[i, xx]
            td[y, xx] = tot
            if core == 0:
                remote(log, td.at[y, xx], XD0.at[o], s_vd.at[o], r_vd.at[o], at(y, xx, 1))
            elif o:
                remote(log, td.at[y, xx], XD1.at[o - 1], s_xd.at[o - 1], r_xd.at[o - 1], at(y, xx, 1))
        for cp in cp_pa:
            cp.wait_recv()

    @pl.when(c == 0)
    def _():
        log, near = [], []
        sum_merged(0, log)
        a = pg[...]
        gram = nt(a, a, HI)
        a = eliminate([jnp.concatenate([a[:, :64], gram, jnp.zeros((RANK, 32), F32)], axis=1)], 0, 64)
        left = jnp.where(lane < 64, a, 0.0)
        right = pltpu.roll(left, 64, axis=1)
        w = jnp.concatenate([left, right, left, right], axis=0)
        for o in far_y:
            describe(TU0.at[x, y], YU0.at[o - 1], s_yu.at[o - 1], r_yu.at[o - 1], partner).wait_recv()
        for o in far_y + (0,):
            describe(TU1.at[x, y], YU1.at[o], s_vu.at[o], r_vu.at[o], partner).wait_recv()
        low = TU0[x, y]
        for i in range(NY - 1):
            low = low + YU0[i]
        high = YU1[0]
        for i in range(1, NY):
            high = high + YU1[i]
        r = nt(jnp.concatenate([low, high], axis=0) * (1.0 / 64.0), w, HI)
        SA1[...] = jnp.where(lane16 < 64, r[16:32], jnp.concatenate([r[48:56], jnp.zeros((8, 128), F32)], axis=0))
        SA0[...] = jnp.where(lane16 < 64, r[0:16], r[32:48])

        cp_ay = []
        for o in far_y:
            remote(log, SA1, FA1.at[x, y], s_a1.at[o], r_a1.at[o], at(ys[o], x, 1))
            cp_ay.append(remote(log, SA0, FA0.at[x, y], s_ay.at[o - 1], r_ay.at[o - 1], ypeer(o)))
        remote(log, SA1, FA1.at[x, y], s_a1.at[0], r_a1.at[0], partner)
        local(near, SA0, FA0.at[x, y], own_sem.at[0])
        SW[...] = w.T
        remote(log, SW, wu_out, s_wu, r_wu, partner)
        local(near, SW, wu_out, own_sem.at[1])
        near[0].wait()
        for cp in cp_ay:
            cp.wait_recv()
        cp_ax = [remote(log, FA0.at[x], FA0.at[x], s_ax.at[o - 1], r_ax.at[o - 1], xpeer(o)) for o in far_x]
        remote(log, FA0.at[x], FA0.at[x], s_ac.at[0], r_ac.at[0], partner)
        for cp, o in zip(cp_ax, far_x):
            cp.wait_recv()
            xx = xof(NX - o)
            remote(log, FA0.at[xx], FA0.at[xx], s_ac.at[o], r_ac.at[o], partner)
        describe(SW, wd_out, s_wd, r_wd, partner).wait_recv()
        for o in range(NY):
            describe(FB.at[ys[o]], FB.at[ys[o]], s_bc.at[o], r_bc.at[o], partner).wait_recv()
        for o in range(NX):
            describe(FA1.at[xs[o]], FA1.at[xs[o]], s_ad.at[o], r_ad.at[o], partner).wait_recv()
        for cp in log:
            cp.wait_send()
        near[1].wait()

    @pl.when(c == 1)
    def _():
        log, near = [], []
        sum_merged(1, log)
        a = pg[...]
        gram = nt(a, a, HI)
        a = eliminate([a, jnp.concatenate([gram, jnp.zeros((RANK, 96), F32)], axis=1)], 1, 0)
        w = jnp.concatenate([a, a, a, a], axis=0)
        for o in far_x:
            describe(TD1.at[y, x], XD1.at[o - 1], s_xd.at[o - 1], r_xd.at[o - 1], partner).wait_recv()
        for o in far_x + (0,):
            describe(TD0.at[y, x], XD0.at[o], s_vd.at[o], r_vd.at[o], partner).wait_recv()
        low = (XD0[0] + XD0[1]) + (XD0[2] + XD0[3])
        high = (TD1[y, x] + XD1[0]) + (XD1[1] + XD1[2])
        r = nt(jnp.concatenate([low, high], axis=0) * (1.0 / 64.0), w, HI)
        low = jnp.where(lane8 < 32, r[0:8], r[8:16])
        high = jnp.where(lane8 < 96, r[16:24], r[24:32])
        SB[...] = jnp.where(lane8 < 64, low, high)

        cp_bx = [remote(log, SB, FB.at[y, x], s_bx.at[o - 1], r_bx.at[o - 1], xpeer(o)) for o in far_x]
        local(near, SB, FB.at[y, x], own_sem.at[0])
        SW[...] = w.T
        remote(log, SW, wd_out, s_wd, r_wd, partner)
        local(near, SW, wd_out, own_sem.at[1])
        near[0].wait()
        for cp in cp_bx:
            cp.wait_recv()
        cp_by = [remote(log, FB.at[y], FB.at[y], s_by.at[o - 1], r_by.at[o - 1], ypeer(o)) for o in far_y]
        remote(log, FB.at[y], FB.at[y], s_bc.at[0], r_bc.at[0], partner)
        for o in (0,) + far_y:
            describe(SA1, FA1.at[x, yof(NY - o)], s_a1.at[o], r_a1.at[o], partner).wait_recv()
        cp_ax = [remote(log, FA1.at[x], FA1.at[x], s_ax.at[o - 1], r_ax.at[o - 1], xpeer(o)) for o in far_x]
        remote(log, FA1.at[x], FA1.at[x], s_ad.at[0], r_ad.at[0], partner)
        for cp, o in zip(cp_by, far_y):
            cp.wait_recv()
            yy = yof(NY - o)
            remote(log, FB.at[yy], FB.at[yy], s_bc.at[o], r_bc.at[o], partner)
        for cp, o in zip(cp_ax, far_x):
            cp.wait_recv()
            xx = xof(NX - o)
            remote(log, FA1.at[xx], FA1.at[xx], s_ad.at[o], r_ad.at[o], partner)
        describe(SW, wu_out, s_wu, r_wu, partner).wait_recv()
        for o in range(NX):
            describe(FA0.at[xs[o]], FA0.at[xs[o]], s_ac.at[o], r_ac.at[o], partner).wait_recv()
        for cp in log:
            cp.wait_send()
        near[1].wait()

    for cp in sent:
        cp.wait_send()


def finish(fa0, fa1, fb, wu, wd, ug, ue, dg, de, ua, ur, da, dr, bua, bur, bda, bdr, sem):
    lane = lax.broadcasted_iota(jnp.int32, (8, 128), 1)
    started = []

    def store(src, dst, cols):
        cp = pltpu.make_async_copy(src.at[:, cols], dst.at[:, cols], sem.at[len(started)])
        cp.start()
        started.append(cp)

    def up_tile(tile):
        q, u = tile // 7, tile % 7
        src, r0 = (fa0, fa1)[u % 4 // 2], (u % 2) * 8
        return jnp.where(lane // 64 == u // 4, src[q // NY, q % NY, r0:r0 + 8, :], 0.0)

    def down_tile(tile):
        q, u = tile // 4, tile % 4
        return jnp.where(lane // 32 == u, fb[q // NX, q % NX], 0.0)

    for first, last in ((0, 2), (2, 4), (4, 6), (6, 7)):
        for b in range(first, last):
            delta = nt3(wu[...], jnp.concatenate([up_tile(32 * b + i) for i in range(32)], axis=0))
            for half in range(2):
                cols = pl.ds(half * HALF + 256 * b, 256)
                part = delta[64 * half:64 * half + 64, :]
                bua[:, cols] = part.astype(BF16)
                bur[:, cols] = (ug[:, cols].astype(F32) + ue[:, cols]) - part
        for half in range(2):
            cols = pl.ds(half * HALF + 256 * first, 256 * (last - first))
            store(bua, ua, cols)
            store(bur, ur, cols)
    for first, last in ((0, 2), (2, 4)):
        for b in range(first, last):
            cols = pl.ds(256 * b, 256)
            delta = nt3(wd[...], jnp.concatenate([down_tile(32 * b + i) for i in range(32)], axis=0))
            bda[:, cols] = delta.astype(BF16)
            bdr[:, cols] = (dg[:, cols].astype(F32) + de[:, cols]) - delta
        cols = pl.ds(256 * first, 256 * (last - first))
        store(bda, da, cols)
        store(bdr, dr, cols)
    for cp in started:
        cp.wait()


def body(up_grad, up_error, up_warm, down_grad, down_error, down_warm):
    ug, ue, dg, de = up_grad[0], up_error[0], down_grad[0], down_error[0]
    vm = pl.BlockSpec(memory_space=pltpu.VMEM)
    hbm = pl.BlockSpec(memory_space=pltpu.HBM)
    anywhere = pl.BlockSpec(memory_space=pl.ANY)
    dma = pltpu.SemaphoreType.DMA
    V = pltpu.VMEM
    fa0, fa1, fb, wu, wd = pl.pallas_call(
        exchange,
        out_shape=(
            jax.ShapeDtypeStruct((NX, NY, 16, 128), F32),
            jax.ShapeDtypeStruct((NX, NY, 16, 128), F32),
            jax.ShapeDtypeStruct((NY, NX, 8, 128), F32),
            jax.ShapeDtypeStruct((128, 128), F32),
            jax.ShapeDtypeStruct((128, 128), F32),
        ),
        in_specs=[hbm] * 6,
        out_specs=(anywhere,) * 5,
        scratch_shapes=[
            V((UP_R, UP_C), BF16), V((UP_R, UP_C), F32), V((RANK, UP_C), F32),
            V((DN_R, DN_C), BF16), V((DN_R, DN_C), F32), V((RANK, DN_C), F32),
            V((NX, NY, 32, 128), F32), V((NX, NY, 24, 128), F32), V((NY, NX, 16, 128), F32), V((NY, NX, 16, 128), F32),
            V((NX, NY, 32, 128), F32), V((NX, NY, 24, 128), F32), V((NY, NX, 16, 128), F32),
            V((NX - 1, NY, 32, 128), F32), V((NX - 1, NY, 24, 128), F32), V((NY - 1, NX, 16, 128), F32),
            V((NY - 1, 32, 128), F32), V((NY, 24, 128), F32), V((NX, 16, 128), F32), V((NX - 1, 16, 128), F32),
            V((16, 128), F32), V((16, 128), F32), V((8, 128), F32), V((128, 128), F32),
            V((64, 128), F32), V((32, 128), F32), V((32, 128), F32), V((3, 8, 128), F32),
            V((NZ, 8, 128), F32), V((NY, 8, 128), F32), V((32, 128), F32),
            dma((9,)), *[dma((n,)) for n in (4, 4, 8, 8, 3, 3, 7, 7, 7, 7, 3, 3, 8, 8, 4, 4)],
            *[dma((n,)) for n in (3, 3, 7, 7, 7, 7, 3, 3)],
            *[dma((n,)) for n in (7, 7, 8, 8, 3, 3, 4, 4, 4, 4, 3, 3, 7, 7, 8, 8)], dma((2,)),
            *[dma] * 6,
        ],
        compiler_params=pltpu.CompilerParams(
            collective_id=0, has_side_effects=True, vmem_limit_bytes=32 * 1024 * 1024),
        name="exchange",
    )(*[pltpu.with_memory_space_constraint(a, pltpu.HBM) for a in (ug, ue, up_warm.T, dg, de, down_warm.T)])
    ua, ur, da, dr = pl.pallas_call(
        finish,
        out_shape=(
            jax.ShapeDtypeStruct((UP_R, UP_C), BF16),
            jax.ShapeDtypeStruct((UP_R, UP_C), F32),
            jax.ShapeDtypeStruct((DN_R, DN_C), BF16),
            jax.ShapeDtypeStruct((DN_R, DN_C), F32),
        ),
        in_specs=[vm] * 9,
        out_specs=(anywhere,) * 4,
        scratch_shapes=[
            V((UP_R, UP_C), BF16), V((UP_R, UP_C), F32), V((DN_R, DN_C), BF16), V((DN_R, DN_C), F32), dma((20,)),
        ],
        compiler_params=pltpu.CompilerParams(vmem_limit_bytes=32 * 1024 * 1024),
        name="finish",
    )(fa0, fa1, fb, wu, wd, ug, ue, dg, de)
    return ua, ur[None], da, dr[None]


def solution(mesh):
    return jax.shard_map(
        body,
        mesh=mesh,
        in_specs=(
            P("dp", None, "mp"),
            P("dp", None, "mp"),
            P("mp", None),
            P("dp", None, "mp"),
            P("dp", None, "mp"),
            P("mp", None),
        ),
        out_specs=(P(None, "mp"), P("dp", None, "mp"), P(None, "mp"), P("dp", None, "mp")),
        check_vma=False,
    )
```

time: 515 us -> 49.3 us (0.10)
  blocking collectives: 279 us -> 0 us
  waiting for transfers between devices: 194 us -> 0 us
  Pallas kernels: 0 us -> 48.5 us
  between operations: 14.2 us -> 0.7 us
  other arithmetic: 13.4 us -> 0 us
  matrix products: 11.4 us -> 0 us
    psum x2 -> x0, blocking collectives: 279 us -> none  [the longest x1 249 us: body(): up_proj, down_proj = lax.psum((up_proj, down_proj), 'dp')]
    psum x1 -> x0, waiting for transfers between devices: 194 us -> none  [body(): up_total, down_total = lax.psum((up_back, down_back), 'dp')]
    pallas_call x0 -> x2, Pallas kernels: none -> 48.5 us  [the longest x1 46.6 us: body(): pl.pallas_call(exchange, out_shape=(jax.ShapeDtypeStruct((NX, NY, 16, 128...]
    another operation x10 -> x0, other arithmetic: 13.4 us -> none  [the longest x6 7.2 us: orthonormal(): chol = jnp.linalg.cholesky(gram)]
    dot_general x8 -> x0, matrix products: 11 us -> none  [the longest x2 4.66 us: expand(): lax.dot_general(ortho, factor, (((1,), (1,)), ((), ())), precision=lax.Pr...]
  transfers between devices with their start and end apart: 1 -> 0, of which waited for: 1 -> 0; matrix products, arithmetic and copies ran while one was open for 0% -> 0% of each run, Pallas kernels for 0% -> 0%
where the time goes in v3:
time: 49.3 us; the launch traced here: 49.2 us
  Pallas kernels  48.5 us (98%)
  between operations  0.7 us (1%)
    pallas_call x1, Pallas kernels, body(): pl.pallas_call(exchange, out_shape=(jax.ShapeDtypeStruct((NX, NY, 16, 128...  46.6 us
    pallas_call x1, Pallas kernels, body(): pl.pallas_call(finish, out_shape=(jax.ShapeDtypeStruct((UP_R, UP_C), BF16...  1.82 us

profile of v3, /device:TPU:1, one launch (start us, length us, event | category | flops | bytes accessed | tf_op | source)
XLA Modules:
  0.0 49.2 jit_solution(12460805895173846680)
XLA Ops:
  0.6 0.0 copy-start
  0.6 0.0 copy-start.1
  0.7 0.0 copy-start.2
  0.7 0.0 copy-start.3
  0.7 46.6 %exchange.1 = (f32[4,8,16,128]{3,2,1,0:T(8,128)S(1)}, f32[4,8,16,128]{3,2,1,0:T(8,128)S(1)}, f32[8,4,8,128]{3,2,1,0:T(8,128)S(1)}, f32[128,128]{1,0:T(8,128)S(1)}, f32[128,128]{1,0:T(8,128)S(1)}) custom-call(bf16[64,3584]{1,0:T(8,128)(2,1)} %bitcast.12, f32[64,3584]{1,0:T(8,128)} %bitcast.8, f32[32,3584]{1,0:T(8,128)} %bitcast.16, ...), custom_call_target="tpu_custom_call" | custom-call | tf_op jit(solution)/shard_map/exchange/pallas_call | solution.py:407
  47.3 0.0 copy-done
  47.3 0.0 copy-done.1
  47.3 0.0 copy-done.2
  47.4 0.0 copy-done.3
  47.4 1.8 %finish.1 = (bf16[64,3584]{1,0:T(8,128)(2,1)}, f32[64,3584]{1,0:T(8,128)}, bf16[128,1024]{1,0:T(8,128)(2,1)}, f32[128,1024]{1,0:T(8,128)}) custom-call(f32[4,8,16,128]{3,2,1,0:T(8,128)S(1)} %get-tuple-element.13.fa0, f32[4,8,16,128]{3,2,1,0:T(8,128)S(1)} %get-tuple-element.14.fa1, f32[8,4,8,128]{3,2,1,0:T(8,128)S(1)} %get-tuple-element.15.fb, ...), custom_call_target="tpu_custom_call" | custom-call | tf_op jit(solution)/shard_map/finish/pallas_call | solution.py:437
Async XLA Ops:
  0.6 46.7 %copy-start = (f32[1,64,3584]{2,1,0:T(8,128)S(1)}, f32[1,64,3584]{2,1,0:T(8,128)}, u32[]{:S(2)}) copy-start(f32[1,64,3584]{2,1,0:T(8,128)} %param.7) | copy-start | bytes 2752516
  0.6 46.7 %copy-start.1 = (f32[1,128,1024]{2,1,0:T(8,128)S(1)}, f32[1,128,1024]{2,1,0:T(8,128)}, u32[]{:S(2)}) copy-start(f32[1,128,1024]{2,1,0:T(8,128)} %param.10) | copy-start | bytes 1572868
  0.7 46.7 %copy-start.2 = (bf16[1,64,3584]{2,1,0:T(8,128)(2,1)S(1)}, bf16[1,64,3584]{2,1,0:T(8,128)(2,1)}, u32[]{:S(2)}) copy-start(bf16[1,64,3584]{2,1,0:T(8,128)(2,1)} %param.6) | copy-start | bytes 1376260
  0.7 46.7 %copy-start.3 = (bf16[1,128,1024]{2,1,0:T(8,128)(2,1)S(1)}, bf16[1,128,1024]{2,1,0:T(8,128)(2,1)}, u32[]{:S(2)}) copy-start(bf16[1,128,1024]{2,1,0:T(8,128)(2,1)} %param.9) | copy-start | bytes 786436

commit v4 on v3

--- a/solution.py
+++ b/solution.py
@@ -29,6 +29,12 @@
     ah, al = split(a)
     bh, bl = split(b)
     return nt(ah, bh) + nt(ah, bl) + nt(al, bh)
+
+
+def nt_acc(acc, wide, a, b):
+    bh, bl = split(b)
+    both = nt(wide, bh)
+    return acc + both[:RANK] + both[RANK:] + nt(a, bl)
 
 
 def eliminate(arrays, where, off):
@@ -48,13 +54,14 @@
     return arrays[0] * scale
 
 
-def exchange(ug, ue, uw, dg, de, dw, FA0, FA1, FB, wu_out, wd_out,
+def exchange(ug, ue, uw, dg, de, dw, FA0, FA1, FB, wu_out, wd_out, mu_out, md_out,
+             MU, MD,
              vug, vue, vuw, vdg, vde, vdw, TU0, TU1, TD0, TD1, CU0, CU1, CD, XU0, XU1, YD, YU0, YU1, XD0, XD1,
-             SA0, SA1, SB, SW, pt, pc, px, pxr, pz, py, pg,
+             SA0, SA1, SB, SW, pt, pxr, pz, py, pg,
              in_sem, s_cu, r_cu, s_cd, r_cd, s_xu, r_xu, s_yd, r_yd, s_yu, r_yu, s_xd, r_xd, s_vu, r_vu, s_vd, r_vd,
              s_px, r_px, s_pz, r_pz, s_py, r_py, s_pa, r_pa,
              s_ay, r_ay, s_a1, r_a1, s_ax, r_ax, s_ac, r_ac, s_ad, r_ad, s_bx, r_bx, s_by, r_by, s_bc, r_bc, own_sem,
-             s_pc, r_pc, s_wu, r_wu, s_wd, r_wd):
+             s_wu, r_wu, s_wd, r_wd):
     d = lax.axis_index("dp")
     z = lax.axis_index("mp")
     c = lax.rem(d, 2)
@@ -94,16 +101,23 @@
         pairs += [(ug.at[:, cols], vug.at[:, cols]), (ue.at[:, cols], vue.at[:, cols]), (uw.at[:, cols], vuw.at[:, cols])]
     pairs += [(dg, vdg), (de, vde), (dw, vdw)]
     loads = [pltpu.make_async_copy(a, b, in_sem.at[i]) for i, (a, b) in enumerate(pairs)]
+    bar = pltpu.get_barrier_semaphore()
+
+    def greet(dev):
+        pl.semaphore_signal(bar, 1, device_id=dev, device_id_type=MESH)
+
+    for o in far_y[:3]:
+        greet(zpeer(o))
+        greet(ypeer(o))
     for cp in loads:
         cp.start()
-
-    bar = pltpu.get_barrier_semaphore()
-    for o in far_y:
-        pl.semaphore_signal(bar, 1, device_id=zpeer(o), device_id_type=MESH)
-        pl.semaphore_signal(bar, 1, device_id=ypeer(o), device_id_type=MESH)
+    for o in far_y[3:]:
+        greet(zpeer(o))
+        greet(ypeer(o))
     for o in far_x:
-        pl.semaphore_signal(bar, 1, device_id=xpeer(o), device_id_type=MESH)
-    pl.semaphore_signal(bar, 1, device_id=partner, device_id_type=MESH)
+        greet(at(y, xs[o], other))
+        greet(xpeer(o))
+    greet(partner)
 
     def down_part(b):
         cols = pl.ds(256 * b, 256)
@@ -118,16 +132,18 @@
         for cp in loads[3 * half:3 * half + 3]:
             cp.wait()
         for b in range(HALF // 256):
-            acc += nt3(vuw[:, pl.ds(half * HALF + 256 * b, 256)], up_part(half, b))
+            hi, lo = split(vuw[:, pl.ds(half * HALF + 256 * b, 256)])
+            acc = nt_acc(acc, jnp.concatenate([hi, lo], axis=0), hi, up_part(half, b))
     pt[0:32, :] = jnp.concatenate([acc, jnp.zeros((RANK, 64), F32)], axis=1)
     for cp in loads[6:]:
         cp.wait()
     acc = jnp.zeros((RANK, DN_R), F32)
     for b in range(DN_C // 256):
-        acc += nt3(vdw[:, pl.ds(256 * b, 256)], down_part(b))
+        hi, lo = split(vdw[:, pl.ds(256 * b, 256)])
+        acc = nt_acc(acc, jnp.concatenate([hi, lo], axis=0), hi, down_part(b))
     pt[32:64, :] = acc
 
-    pl.semaphore_wait(bar, 1 + 7 + 7 + 3)
+    pl.semaphore_wait(bar, 7 + 7 + 7)
 
     def describe(src, dst, ssem, rsem, dev):
         return pltpu.make_async_remote_copy(src_ref=src, dst_ref=dst, send_sem=ssem, recv_sem=rsem,
@@ -140,10 +156,16 @@
         return cp
 
     sent = []
-    cp_pc = remote(sent, pt.at[pl.ds(pl.multiple_of(other * 32, 32), 32)], pc, s_pc, r_pc, partner)
+    cp_px = []
+    for o, cc, k in ((2, other, 5), (2, c, 1), (1, other, 4), (3, other, 6), (1, c, 0), (3, c, 2), (0, other, 3)):
+        rows = pl.ds(pl.multiple_of(cc * 32 + xs[o] * 8, 8), 8)
+        cp_px.append(remote(sent, pt.at[rows], pxr.at[k], s_px.at[k], r_px.at[k], at(y, xs[o], cc)))
 
     for b in range(HALF // 256):
-        stacked = jnp.concatenate([up_part(0, b), up_part(1, b)], axis=0)
+        parts = [up_part(0, b), up_part(1, b)]
+        for half in range(2):
+            MU[:, half * HALF + 256 * b:half * HALF + 256 * b + 256] = parts[half]
+        stacked = jnp.concatenate(parts, axis=0)
         for s in range(2):
             turned = stacked[:, 128 * s:128 * (s + 1)].T
             for i in range(16):
@@ -152,13 +174,9 @@
                 dst, r0 = (TU0, 8 * u) if u < 4 else (TU1, 8 * u - 32)
                 dst[q // NY, q % NY, r0:r0 + 8, :] = turned[8 * i:8 * i + 8, :]
 
-    cp_pc.wait_recv()
-    px[...] = pt[pl.ds(pl.multiple_of(c * 32, 32), 32), :] + pc[...]
-    cp_px = [remote(sent, px.at[pl.ds(pl.multiple_of(xof(o) * 8, 8), 8)], pxr.at[o - 1],
-                    s_px.at[o - 1], r_px.at[o - 1], xpeer(o)) for o in far_x]
-
     for b in range(DN_C // 256):
         m = down_part(b)
+        MD[:, 256 * b:256 * b + 256] = m
         for s in range(2):
             turned = m[:, 128 * s:128 * (s + 1)].T
             for i in range(4):
@@ -166,12 +184,16 @@
                 TD0[q // NX, q % NX] = turned[32 * i:32 * i + 16, :]
                 TD1[q // NX, q % NX] = turned[32 * i + 16:32 * i + 32, :]
 
+    keep = [pltpu.make_async_copy(MU, mu_out, own_sem.at[2]), pltpu.make_async_copy(MD, md_out, own_sem.at[3])]
+    for cp in keep:
+        cp.start()
     mine = pl.ds(pl.multiple_of(x * 8, 8), 8)
 
     def proj_z(log):
         for cp in cp_px:
             cp.wait_recv()
-        pz[z] = (px[mine, :] + pxr[0]) + (pxr[1] + pxr[2])
+        own = pt[pl.ds(pl.multiple_of(c * 32 + x * 8, 8), 8), :]
+        pz[z] = ((own + pxr[0]) + (pxr[1] + pxr[2])) + ((pxr[3] + pxr[4]) + (pxr[5] + pxr[6]))
         return [remote(log, pz.at[z], pz.at[z], s_pz.at[o - 1], r_pz.at[o - 1], zpeer(o)) for o in far_y]
 
     def proj_y(log, cps):
@@ -251,6 +273,16 @@
         for cp in cp_pa:
             cp.wait_recv()
 
+    def pass_on(log, ref, k):
+        return [remote(log, ref.at[x, ys[k]], ref.at[x, ys[k]], s_ax.at[8 * (o - 1) + k], r_ax.at[8 * (o - 1) + k],
+                       xpeer(o)) for o in far_x]
+
+    def gathered(cps):
+        for cp in cps:
+            cp.wait_recv()
+
+    near_y = (1, 7, 2, 6, 3, 5, 4)
+
     @pl.when(c == 0)
     def _():
         log, near = [], []
@@ -275,22 +307,28 @@
         SA1[...] = jnp.where(lane16 < 64, r[16:32], jnp.concatenate([r[48:56], jnp.zeros((8, 128), F32)], axis=0))
         SA0[...] = jnp.where(lane16 < 64, r[0:16], r[32:48])
 
-        cp_ay = []
+        before = len(log)
+        cp_ay = {}
         for o in far_y:
+            cp_ay[o] = remote(log, SA0, FA0.at[x, y], s_ay.at[o - 1], r_ay.at[o - 1], ypeer(o))
             remote(log, SA1, FA1.at[x, y], s_a1.at[o], r_a1.at[o], at(ys[o], x, 1))
-            cp_ay.append(remote(log, SA0, FA0.at[x, y], s_ay.at[o - 1], r_ay.at[o - 1], ypeer(o)))
         remote(log, SA1, FA1.at[x, y], s_a1.at[0], r_a1.at[0], partner)
         local(near, SA0, FA0.at[x, y], own_sem.at[0])
+        near[0].wait()
+        pieces = [pass_on(log, FA0, 0)]
+        for k in near_y:
+            cp_ay[NY - k].wait_recv()
+            pieces.append(pass_on(log, FA0, k))
+        remote(log, FA0.at[x], FA0.at[x], s_ac.at[0], r_ac.at[0], partner)
         SW[...] = w.T
         remote(log, SW, wu_out, s_wu, r_wu, partner)
         local(near, SW, wu_out, own_sem.at[1])
-        near[0].wait()
-        for cp in cp_ay:
-            cp.wait_recv()
-        cp_ax = [remote(log, FA0.at[x], FA0.at[x], s_ax.at[o - 1], r_ax.at[o - 1], xpeer(o)) for o in far_x]
-        remote(log, FA0.at[x], FA0.at[x], s_ac.at[0], r_ac.at[0], partner)
-        for cp, o in zip(cp_ax, far_x):
-            cp.wait_recv()
+        for cp in sent + log[:before]:
+            cp.wait_send()
+        for cp in keep:
+            cp.wait()
+        for i, o in ((1, 1), (2, 3), (0, 2)):
+            gathered([p[i] for p in pieces])
             xx = xof(NX - o)
             remote(log, FA0.at[xx], FA0.at[xx], s_ac.at[o], r_ac.at[o], partner)
         describe(SW, wd_out, s_wd, r_wd, partner).wait_recv()
@@ -298,7 +336,7 @@
             describe(FB.at[ys[o]], FB.at[ys[o]], s_bc.at[o], r_bc.at[o], partner).wait_recv()
         for o in range(NX):
             describe(FA1.at[xs[o]], FA1.at[xs[o]], s_ad.at[o], r_ad.at[o], partner).wait_recv()
-        for cp in log:
+        for cp in log[before:]:
             cp.wait_send()
         near[1].wait()
 
@@ -321,6 +359,7 @@
         high = jnp.where(lane8 < 96, r[16:24], r[24:32])
         SB[...] = jnp.where(lane8 < 64, low, high)
 
+        before = len(log)
         cp_bx = [remote(log, SB, FB.at[y, x], s_bx.at[o - 1], r_bx.at[o - 1], xpeer(o)) for o in far_x]
         local(near, SB, FB.at[y, x], own_sem.at[0])
         SW[...] = w.T
@@ -330,31 +369,34 @@
         for cp in cp_bx:
             cp.wait_recv()
         cp_by = [remote(log, FB.at[y], FB.at[y], s_by.at[o - 1], r_by.at[o - 1], ypeer(o)) for o in far_y]
+        pieces = []
+        for k in (0,) + near_y:
+            o = (NY - k) % NY
+            describe(SA1, FA1.at[x, ys[k]], s_a1.at[o], r_a1.at[o], partner).wait_recv()
+            pieces.append(pass_on(log, FA1, k))
+        remote(log, FA1.at[x], FA1.at[x], s_ad.at[0], r_ad.at[0], partner)
         remote(log, FB.at[y], FB.at[y], s_bc.at[0], r_bc.at[0], partner)
-        for o in (0,) + far_y:
-            describe(SA1, FA1.at[x, yof(NY - o)], s_a1.at[o], r_a1.at[o], partner).wait_recv()
-        cp_ax = [remote(log, FA1.at[x], FA1.at[x], s_ax.at[o - 1], r_ax.at[o - 1], xpeer(o)) for o in far_x]
-        remote(log, FA1.at[x], FA1.at[x], s_ad.at[0], r_ad.at[0], partner)
+        for cp in sent + log[:before]:
+            cp.wait_send()
+        for cp in keep:
+            cp.wait()
         for cp, o in zip(cp_by, far_y):
             cp.wait_recv()
             yy = yof(NY - o)
             remote(log, FB.at[yy], FB.at[yy], s_bc.at[o], r_bc.at[o], partner)
-        for cp, o in zip(cp_ax, far_x):
-            cp.wait_recv()
+        for i, o in ((1, 1), (2, 3), (0, 2)):
+            gathered([p[i] for p in pieces])
             xx = xof(NX - o)
             remote(log, FA1.at[xx], FA1.at[xx], s_ad.at[o], r_ad.at[o], partner)
         describe(SW, wu_out, s_wu, r_wu, partner).wait_recv()
         for o in range(NX):
             describe(FA0.at[xs[o]], FA0.at[xs[o]], s_ac.at[o], r_ac.at[o], partner).wait_recv()
-        for cp in log:
+        for cp in log[before:]:
             cp.wait_send()
         near[1].wait()
 
-    for cp in sent:
-        cp.wait_send()
-
-
-def finish(fa0, fa1, fb, wu, wd, ug, ue, dg, de, ua, ur, da, dr, bua, bur, bda, bdr, sem):
+
+def finish(fa0, fa1, fb, wu, wd, mu, md, ua, ur, da, dr, bua, bur, bda, bdr, sem):
     lane = lax.broadcasted_iota(jnp.int32, (8, 128), 1)
     started = []
 
@@ -379,7 +421,7 @@
                 cols = pl.ds(half * HALF + 256 * b, 256)
                 part = delta[64 * half:64 * half + 64, :]
                 bua[:, cols] = part.astype(BF16)
-                bur[:, cols] = (ug[:, cols].astype(F32) + ue[:, cols]) - part
+                bur[:, cols] = mu[:, cols] - part
         for half in range(2):
             cols = pl.ds(half * HALF + 256 * first, 256 * (last - first))
             store(bua, ua, cols)
@@ -389,7 +431,7 @@
             cols = pl.ds(256 * b, 256)
             delta = nt3(wd[...], jnp.concatenate([down_tile(32 * b + i) for i in range(32)], axis=0))
             bda[:, cols] = delta.astype(BF16)
-            bdr[:, cols] = (dg[:, cols].astype(F32) + de[:, cols]) - delta
+            bdr[:, cols] = md[:, cols] - delta
         cols = pl.ds(256 * first, 256 * (last - first))
         store(bda, da, cols)
         store(bdr, dr, cols)
@@ -404,7 +446,7 @@
     anywhere = pl.BlockSpec(memory_space=pl.ANY)
     dma = pltpu.SemaphoreType.DMA
     V = pltpu.VMEM
-    fa0, fa1, fb, wu, wd = pl.pallas_call(
+    fa0, fa1, fb, wu, wd, mu, md = pl.pallas_call(
         exchange,
         out_shape=(
             jax.ShapeDtypeStruct((NX, NY, 16, 128), F32),
@@ -412,10 +454,13 @@
             jax.ShapeDtypeStruct((NY, NX, 8, 128), F32),
             jax.ShapeDtypeStruct((128, 128), F32),
             jax.ShapeDtypeStruct((128, 128), F32),
+            jax.ShapeDtypeStruct((UP_R, UP_C), F32),
+            jax.ShapeDtypeStruct((DN_R, DN_C), F32),
         ),
         in_specs=[hbm] * 6,
-        out_specs=(anywhere,) * 5,
+        out_specs=(anywhere,) * 7,
         scratch_shapes=[
+            V((UP_R, UP_C), F32), V((DN_R, DN_C), F32),
             V((UP_R, UP_C), BF16), V((UP_R, UP_C), F32), V((RANK, UP_C), F32),
             V((DN_R, DN_C), BF16), V((DN_R, DN_C), F32), V((RANK, DN_C), F32),
             V((NX, NY, 32, 128), F32), V((NX, NY, 24, 128), F32), V((NY, NX, 16, 128), F32), V((NY, NX, 16, 128), F32),
@@ -423,12 +468,12 @@
             V((NX - 1, NY, 32, 128), F32), V((NX - 1, NY, 24, 128), F32), V((NY - 1, NX, 16, 128), F32),
             V((NY - 1, 32, 128), F32), V((NY, 24, 128), F32), V((NX, 16, 128), F32), V((NX - 1, 16, 128), F32),
             V((16, 128), F32), V((16, 128), F32), V((8, 128), F32), V((128, 128), F32),
-            V((64, 128), F32), V((32, 128), F32), V((32, 128), F32), V((3, 8, 128), F32),
+            V((64, 128), F32), V((7, 8, 128), F32),
             V((NZ, 8, 128), F32), V((NY, 8, 128), F32), V((32, 128), F32),
             dma((9,)), *[dma((n,)) for n in (4, 4, 8, 8, 3, 3, 7, 7, 7, 7, 3, 3, 8, 8, 4, 4)],
-            *[dma((n,)) for n in (3, 3, 7, 7, 7, 7, 3, 3)],
-            *[dma((n,)) for n in (7, 7, 8, 8, 3, 3, 4, 4, 4, 4, 3, 3, 7, 7, 8, 8)], dma((2,)),
-            *[dma] * 6,
+            *[dma((n,)) for n in (7, 7, 7, 7, 7, 7, 3, 3)],
+            *[dma((n,)) for n in (7, 7, 8, 8, 24, 24, 4, 4, 4, 4, 3, 3, 7, 7, 8, 8)], dma((4,)),
+            *[dma] * 4,
         ],
         compiler_params=pltpu.CompilerParams(
             collective_id=0, has_side_effects=True, vmem_limit_bytes=32 * 1024 * 1024),
@@ -442,14 +487,14 @@
             jax.ShapeDtypeStruct((DN_R, DN_C), BF16),
             jax.ShapeDtypeStruct((DN_R, DN_C), F32),
         ),
-        in_specs=[vm] * 9,
+        in_specs=[vm] * 7,
         out_specs=(anywhere,) * 4,
         scratch_shapes=[
             V((UP_R, UP_C), BF16), V((UP_R, UP_C), F32), V((DN_R, DN_C), BF16), V((DN_R, DN_C), F32), dma((20,)),
         ],
         compiler_params=pltpu.CompilerParams(vmem_limit_bytes=32 * 1024 * 1024),
         name="finish",
-    )(fa0, fa1, fb, wu, wd, ug, ue, dg, de)
+    )(fa0, fa1, fb, wu, wd, mu, md)
     return ua, ur[None], da, dr[None]
 
 

time: 49.3 us -> 48.6 us (0.986)
  Pallas kernels: 48.5 us -> 47.8 us
    pallas_call x1, Pallas kernels: 46.6 us -> 46 us  [body(): pl.pallas_call(exchange, out_shape=(jax.ShapeDtypeStruct((NX, NY, 16, 128...]
where the time goes in v4:
time: 48.6 us; the launch traced here: 48.5 us
  Pallas kernels  47.8 us (98%)
  between operations  0.64 us (1%)
    pallas_call x1, Pallas kernels, body(): pl.pallas_call(exchange, out_shape=(jax.ShapeDtypeStruct((NX, NY, 16, 128...  46 us
    pallas_call x1, Pallas kernels, body(): pl.pallas_call(finish, out_shape=(jax.ShapeDtypeStruct((UP_R, UP_C), BF16...  1.82 us

profile of v4, /device:TPU:1, one launch (start us, length us, event | category | flops | bytes accessed | tf_op | source)
XLA Modules:
  0.0 48.5 jit_solution(15007494799639595503)
XLA Ops:
  0.6 46.0 %exchange.1 = (f32[4,8,16,128]{3,2,1,0:T(8,128)S(1)}, f32[4,8,16,128]{3,2,1,0:T(8,128)S(1)}, f32[8,4,8,128]{3,2,1,0:T(8,128)S(1)}, f32[128,128]{1,0:T(8,128)S(1)...) custom-call(bf16[64,3584]{1,0:T(8,128)(2,1)} %bitcast.10, f32[64,3584]{1,0:T(8,128)} %bitcast.8, ...), custom_call_target="tpu_custom_call" | custom-call | tf_op jit(solution)/shard_map/exchange/pallas_call | solution.py:449
  46.7 1.8 %finish.1 = (bf16[64,3584]{1,0:T(8,128)(2,1)}, f32[64,3584]{1,0:T(8,128)}, bf16[128,1024]{1,0:T(8,128)(2,1)}, f32[128,1024]{1,0:T(8,128)}) custom-call(f32[4,8,16,128]{3,2,1,0:T(8,128)S(1)} %get-tuple-element.15.fa0, f32[4,8,16,128]{3,2,1,0:T(8,128)S(1)} %get-tuple-element.16.fa1, f32[8,4,8,128]{3,2,1,0:T(8,128)S(1)} %get-tuple-element.17.fb, ...), custom_call_target="tpu_custom_call" | custom-call | tf_op jit(solution)/shard_map/finish/pallas_call | solution.py:482

commit v5 on v4

--- a/solution.py
+++ b/solution.py
@@ -366,14 +366,15 @@
         remote(log, SW, wd_out, s_wd, r_wd, partner)
         local(near, SW, wd_out, own_sem.at[1])
         near[0].wait()
-        for cp in cp_bx:
-            cp.wait_recv()
-        cp_by = [remote(log, FB.at[y], FB.at[y], s_by.at[o - 1], r_by.at[o - 1], ypeer(o)) for o in far_y]
         pieces = []
         for k in (0,) + near_y:
             o = (NY - k) % NY
             describe(SA1, FA1.at[x, ys[k]], s_a1.at[o], r_a1.at[o], partner).wait_recv()
             pieces.append(pass_on(log, FA1, k))
+            if k == 7:
+                for cp in cp_bx:
+                    cp.wait_recv()
+                cp_by = [remote(log, FB.at[y], FB.at[y], s_by.at[p - 1], r_by.at[p - 1], ypeer(p)) for p in far_y]
         remote(log, FA1.at[x], FA1.at[x], s_ad.at[0], r_ad.at[0], partner)
         remote(log, FB.at[y], FB.at[y], s_bc.at[0], r_bc.at[0], partner)
         for cp in sent + log[:before]:

time: 48.6 us -> 47.7 us (0.981)
  Pallas kernels: 47.8 us -> 46.9 us
    pallas_call x1, Pallas kernels: 46 us -> 45.1 us  [body(): pl.pallas_call(exchange, out_shape=(jax.ShapeDtypeStruct((NX, NY, 16, 128...]
where the time goes in v5:
time: 47.7 us; the launch traced here: 47.6 us
  Pallas kernels  46.9 us (98%)
  between operations  0.64 us (1%)
    pallas_call x1, Pallas kernels, body(): pl.pallas_call(exchange, out_shape=(jax.ShapeDtypeStruct((NX, NY, 16, 128...  45.1 us
    pallas_call x1, Pallas kernels, body(): pl.pallas_call(finish, out_shape=(jax.ShapeDtypeStruct((UP_R, UP_C), BF16...  1.82 us

profile of v5, /device:TPU:1, one launch (start us, length us, event | category | flops | bytes accessed | tf_op | source)
XLA Modules:
  0.0 47.6 jit_solution(10628222640413426240)
XLA Ops:
  0.6 45.1 %exchange.1 = (f32[4,8,16,128]{3,2,1,0:T(8,128)S(1)}, f32[4,8,16,128]{3,2,1,0:T(8,128)S(1)}, f32[8,4,8,128]{3,2,1,0:T(8,128)S(1)}, f32[128,128]{1,0:T(8,128)S(1)...) custom-call(bf16[64,3584]{1,0:T(8,128)(2,1)} %bitcast.10, f32[64,3584]{1,0:T(8,128)} %bitcast.8, ...), custom_call_target="tpu_custom_call" | custom-call | tf_op jit(solution)/shard_map/exchange/pallas_call | solution.py:450
  45.7 1.8 %finish.1 = (bf16[64,3584]{1,0:T(8,128)(2,1)}, f32[64,3584]{1,0:T(8,128)}, bf16[128,1024]{1,0:T(8,128)(2,1)}, f32[128,1024]{1,0:T(8,128)}) custom-call(f32[4,8,16,128]{3,2,1,0:T(8,128)S(1)} %get-tuple-element.15.fa0, f32[4,8,16,128]{3,2,1,0:T(8,128)S(1)} %get-tuple-element.16.fa1, f32[8,4,8,128]{3,2,1,0:T(8,128)S(1)} %get-tuple-element.17.fb, ...), custom_call_target="tpu_custom_call" | custom-call | tf_op jit(solution)/shard_map/finish/pallas_call | solution.py:483

commit v6 on v5

--- a/solution.py
+++ b/solution.py
@@ -309,10 +309,10 @@
 
         before = len(log)
         cp_ay = {}
+        remote(log, SA1, FA1.at[x, y], s_a1.at[0], r_a1.at[0], partner)
         for o in far_y:
+            remote(log, SA1, FA1.at[x, y], s_a1.at[o], r_a1.at[o], at(ys[o], x, 1))
             cp_ay[o] = remote(log, SA0, FA0.at[x, y], s_ay.at[o - 1], r_ay.at[o - 1], ypeer(o))
-            remote(log, SA1, FA1.at[x, y], s_a1.at[o], r_a1.at[o], at(ys[o], x, 1))
-        remote(log, SA1, FA1.at[x, y], s_a1.at[0], r_a1.at[0], partner)
         local(near, SA0, FA0.at[x, y], own_sem.at[0])
         near[0].wait()
         pieces = [pass_on(log, FA0, 0)]

time: 47.7 us -> 47.6 us (level)
  no operation moved by 1% of the time
where the time goes in v6:
time: 47.6 us; the launch traced here: 47.5 us
  Pallas kernels  46.8 us (98%)
  between operations  0.64 us (1%)
    pallas_call x1, Pallas kernels, body(): pl.pallas_call(exchange, out_shape=(jax.ShapeDtypeStruct((NX, NY, 16, 128...  45 us
    pallas_call x1, Pallas kernels, body(): pl.pallas_call(finish, out_shape=(jax.ShapeDtypeStruct((UP_R, UP_C), BF16...  1.82 us

profile of v6, /device:TPU:1, one launch (start us, length us, event | category | flops | bytes accessed | tf_op | source)
XLA Modules:
  0.0 47.5 jit_solution(12766399363227886698)
XLA Ops:
  0.6 45.0 %exchange.1 = (f32[4,8,16,128]{3,2,1,0:T(8,128)S(1)}, f32[4,8,16,128]{3,2,1,0:T(8,128)S(1)}, f32[8,4,8,128]{3,2,1,0:T(8,128)S(1)}, f32[128,128]{1,0:T(8,128)S(1)...) custom-call(bf16[64,3584]{1,0:T(8,128)(2,1)} %bitcast.10, f32[64,3584]{1,0:T(8,128)} %bitcast.8, ...), custom_call_target="tpu_custom_call" | custom-call | tf_op jit(solution)/shard_map/exchange/pallas_call | solution.py:450
  45.7 1.8 %finish.1 = (bf16[64,3584]{1,0:T(8,128)(2,1)}, f32[64,3584]{1,0:T(8,128)}, bf16[128,1024]{1,0:T(8,128)(2,1)}, f32[128,1024]{1,0:T(8,128)}) custom-call(f32[4,8,16,128]{3,2,1,0:T(8,128)S(1)} %get-tuple-element.15.fa0, f32[4,8,16,128]{3,2,1,0:T(8,128)S(1)} %get-tuple-element.16.fa1, f32[8,4,8,128]{3,2,1,0:T(8,128)S(1)} %get-tuple-element.17.fb, ...), custom_call_target="tpu_custom_call" | custom-call | tf_op jit(solution)/shard_map/finish/pallas_call | solution.py:483
